TPU v7x, 32 devices: a whole 2x2x4 slice. The times are simulated.
32 devices in a mesh: section: 4 (over x, core), expert: 8 (over z, y).
Axes of the slice: x: 2, y: 2, z: 4, core: 2. Of those that a mesh axis runs over, the one named last changes fastest.
Arguments:
- inputs: bfloat16 [4, 256, 4096], P(None, 'expert'), may hold values from -6 to 6
- cotangent: bfloat16 [4, 256, 4096], P(None, 'expert'), may hold values from -6 to 6
- gain: float32 [4, 4096], P('section'), may hold values from 0.25 to 1.75
- route: int32 [4, 4, 256, 2], P('section', None, 'expert'), may hold values from 0 to 7, all different within a row; in each aligned block of 32 rows (0 to 31, 32 to 63, ..., all dimensions but the last counted through in order) at most 9 rows name the same one
- gate: float32 [4, 4, 256, 2], P('section', None, 'expert'), may hold values from 0.3 to 1
- w_gate: bfloat16 [4, 8, 4096, 768], P('section', 'expert'), may hold values from -0.09375 to 0.09375
- w_up: bfloat16 [4, 8, 4096, 768], P('section', 'expert'), may hold values from -0.09375 to 0.09375
- w_down: bfloat16 [4, 8, 768, 4096], P('section', 'expert'), may hold values from -0.21875 to 0.21875
Outputs:
- hidden: bfloat16 [4, 4, 256, 4096], P('section', None, 'expert')
- grads: bfloat16 [4, 4, 256, 4096], P('section', None, 'expert')
Inputs may be any that keep to these rules, and one draw needn't show every extreme that they name: `route`: each token names 2 different experts. Among the 32 tokens that one device holds of one micro-batch in one section, no expert is named by more than 9 tokens, a bound that some block reaches.
All inputs are finite; a program needn't handle non-finite values.
Results may differ from a plain program's by a relative error of at most 0.03.
Values may be sent and summed in bfloat16 or wider, within the bound.
A program may use at most 64 MiB of HBM per device.

v0:
```python
import jax
import jax.numpy as jnp
from jax import lax
from jax.sharding import PartitionSpec as P

EPS = 1e-06


def passed_along(value, axis, steps):
    count = lax.axis_size(axis)
    leading, last = (max(0, -steps), min(count, count - steps))
    return lax.ppermute(value, axis, [(source, source + steps) for source in range(leading, last)])


def slot_places(route, experts, capacity):
    flat = route.reshape(-1)
    onehot = (flat[:, None] == jnp.arange(experts, dtype=jnp.int32)[None, :]).astype(jnp.int32)
    before = jnp.cumsum(onehot, axis=0) - onehot
    slot = jnp.sum(before * onehot, axis=1)
    return (flat * capacity + slot).reshape(route.shape)


def slot_table(places, total_rows):
    grid = jnp.arange(total_rows, dtype=jnp.int32)
    return (places.T[:, :, None] == grid[None, None, :]).astype(jnp.bfloat16)


def normalize(tokens, gain):
    values = tokens.astype(jnp.float32)
    scale = lax.rsqrt(jnp.mean(values * values, axis=-1, keepdims=True) + EPS)
    return (values, scale, (values * scale * gain).astype(jnp.bfloat16))


def pre_products(rows, w_gate, w_up):
    flat = rows.reshape(-1, rows.shape[-1])
    pre_gate = jnp.dot(flat, w_gate, preferred_element_type=jnp.float32)
    pre_up = jnp.dot(flat, w_up, preferred_element_type=jnp.float32)
    inner = rows.shape[:-1] + (w_gate.shape[1],)
    return (pre_gate.reshape(inner), pre_up.reshape(inner))


def expert_forward(rows, w_gate, w_up, w_down):
    pre_gate, pre_up = pre_products(rows, w_gate, w_up)
    width = w_gate.shape[1]
    product = (pre_gate * jax.nn.sigmoid(pre_gate) * pre_up).astype(jnp.bfloat16)
    output = jnp.dot(product.reshape(-1, width), w_down, preferred_element_type=jnp.float32).astype(
        jnp.bfloat16
    )
    return (output.reshape(rows.shape), pre_gate, pre_up)


def contract_last(left, right):
    return lax.dot_general(
        left, right, (((1,), (1,)), ((), ())), preferred_element_type=jnp.float32
    )


def expert_backward(grad_rows, pre_gate, pre_up, w_gate, w_up, w_down):
    shape = grad_rows.shape
    width = w_gate.shape[1]
    flat = grad_rows.reshape(-1, shape[-1])
    gate_pre = pre_gate.reshape(-1, width)
    up_pre = pre_up.reshape(-1, width)
    d_hidden = contract_last(flat, w_down)
    sigma = jax.nn.sigmoid(gate_pre)
    d_gate = (d_hidden * up_pre * sigma * (1.0 + gate_pre * (1.0 - sigma))).astype(jnp.bfloat16)
    d_up = (d_hidden * gate_pre * sigma).astype(jnp.bfloat16)
    back = contract_last(d_gate, w_gate) + contract_last(d_up, w_up)
    return back.astype(jnp.bfloat16).reshape(shape)


def return_rows(rows):
    return lax.all_to_all(rows, "expert", split_axis=0, concat_axis=0, tiled=True)


def local(inputs, cotangent, gain, route, gate, w_gate, w_up, w_down):
    micro, tok, width = inputs.shape
    top = route.shape[-1]
    experts = lax.axis_size("expert")
    capacity = tok * top * 7 // (6 * experts)
    total_rows = experts * capacity
    sections = lax.axis_size("section")
    section = lax.axis_index("section")
    ticks = sections + micro - 1
    gain_row = gain[0]
    weight_gate = w_gate[0, 0]
    weight_up = w_up[0, 0]
    weight_down = w_down[0, 0]
    inner = weight_gate.shape[1]
    routes = route[0]
    gates = gate[0]

    def forward_work(tokens, route_now, gate_now, live):
        values, scale, normed = normalize(tokens, gain_row)
        places = slot_places(route_now, experts, capacity)
        table = slot_table(places, total_rows)
        send = jnp.einsum("ktj,td->jd", table, normed, preferred_element_type=jnp.float32).astype(
            jnp.bfloat16
        )
        send = send.reshape(experts, capacity, width)

        def active(operand):
            return expert_forward(operand, weight_gate, weight_up, weight_down)

        def resting(operand):
            pre_zero = jnp.zeros(operand.shape[:-1] + (inner,), jnp.float32)
            return (jnp.zeros_like(operand), pre_zero, pre_zero)

        output, pre_gate, pre_up = lax.cond(
            live,
            active,
            resting,
            lax.all_to_all(send, "expert", split_axis=0, concat_axis=0, tiled=True),
        )
        back = return_rows(output)
        picked = back.reshape(total_rows, width)[places]
        mixed = values + jnp.sum(gate_now[..., None] * picked.astype(jnp.float32), axis=1)
        return (mixed.astype(jnp.bfloat16), pre_gate, pre_up)

    def forward_tick(carry, tick):
        incoming, outputs, kept_x, kept_gate, kept_up = carry
        offset = tick - section
        live = (offset >= 0) & (offset < micro)
        index = jnp.clip(offset, 0, micro - 1)
        fresh = lax.dynamic_index_in_dim(inputs, index, 0, keepdims=False)
        tokens = jnp.where(section == 0, fresh, incoming)
        route_now = lax.dynamic_index_in_dim(routes, index, 0, keepdims=False)
        gate_now = lax.dynamic_index_in_dim(gates, index, 0, keepdims=False)
        mixed, pre_gate, pre_up = forward_work(tokens, route_now, gate_now, live)
        old_out = lax.dynamic_index_in_dim(outputs, index, 0, keepdims=False)
        outputs = lax.dynamic_update_index_in_dim(
            outputs, jnp.where(live, mixed, old_out), index, 0
        )
        old_x = lax.dynamic_index_in_dim(kept_x, index, 0, keepdims=False)
        kept_x = lax.dynamic_update_index_in_dim(kept_x, jnp.where(live, tokens, old_x), index, 0)
        old_gate = lax.dynamic_index_in_dim(kept_gate, index, 0, keepdims=False)
        kept_gate = lax.dynamic_update_index_in_dim(
            kept_gate, jnp.where(live, pre_gate, old_gate), index, 0
        )
        old_up = lax.dynamic_index_in_dim(kept_up, index, 0, keepdims=False)
        kept_up = lax.dynamic_update_index_in_dim(
            kept_up, jnp.where(live, pre_up, old_up), index, 0
        )
        incoming = passed_along(mixed, "section", 1)
        return ((incoming, outputs, kept_x, kept_gate, kept_up), None)

    start = (
        jnp.zeros((tok, width), jnp.bfloat16),
        jnp.zeros_like(inputs),
        jnp.zeros_like(inputs),
        jnp.zeros((micro, experts, capacity, inner), jnp.float32),
        jnp.zeros((micro, experts, capacity, inner), jnp.float32),
    )
    finished, _ = lax.scan(forward_tick, start, jnp.arange(ticks, dtype=jnp.int32))
    _, outputs, kept_x, kept_gate, kept_up = finished

    def backward_work(tokens, grad_out, route_now, gate_now, pre_gate, pre_up, live):
        values, scale, normed = normalize(tokens, gain_row)
        places = slot_places(route_now, experts, capacity)
        table = slot_table(places, total_rows)
        scaled = (gate_now[..., None] * grad_out.astype(jnp.float32)[:, None, :]).astype(
            jnp.bfloat16
        )
        grad_send = jnp.einsum(
            "ktj,tkd->jd", table, scaled, preferred_element_type=jnp.float32
        ).astype(jnp.bfloat16)
        grad_send = grad_send.reshape(experts, capacity, width)
        arrived = lax.all_to_all(grad_send, "expert", split_axis=0, concat_axis=0, tiled=True)

        def active_saved(operands):
            return expert_backward(
                operands[0], operands[1], operands[2], weight_gate, weight_up, weight_down
            )

        def resting_saved(operands):
            return jnp.zeros_like(operands[0])

        computed = lax.cond(live, active_saved, resting_saved, (arrived, pre_gate, pre_up))
        back = return_rows(computed)
        d_norm = jnp.sum(back.reshape(total_rows, width)[places].astype(jnp.float32), axis=1)
        weighted = d_norm * gain_row
        result = (
            grad_out.astype(jnp.float32)
            + scale * weighted
            - values * (scale * scale * scale) * jnp.mean(values * weighted, axis=-1, keepdims=True)
        )
        return result.astype(jnp.bfloat16)

    def backward_tick(carry, tick):
        incoming, results = carry
        offset = tick - (sections - 1 - section)
        live = (offset >= 0) & (offset < micro)
        index = jnp.clip(offset, 0, micro - 1)
        fresh = lax.dynamic_index_in_dim(cotangent, index, 0, keepdims=False)
        grad_out = jnp.where(section == sections - 1, fresh, incoming)
        tokens = lax.dynamic_index_in_dim(kept_x, index, 0, keepdims=False)
        route_now = lax.dynamic_index_in_dim(routes, index, 0, keepdims=False)
        gate_now = lax.dynamic_index_in_dim(gates, index, 0, keepdims=False)
        gate_saved = lax.dynamic_index_in_dim(kept_gate, index, 0, keepdims=False)
        up_saved = lax.dynamic_index_in_dim(kept_up, index, 0, keepdims=False)
        result = backward_work(tokens, grad_out, route_now, gate_now, gate_saved, up_saved, live)
        old_result = lax.dynamic_index_in_dim(results, index, 0, keepdims=False)
        results = lax.dynamic_update_index_in_dim(
            results, jnp.where(live, result, old_result), index, 0
        )
        incoming = passed_along(result, "section", -1)
        return ((incoming, results), None)

    done, _ = lax.scan(
        backward_tick,
        (jnp.zeros((tok, width), jnp.bfloat16), jnp.zeros_like(cotangent)),
        jnp.arange(ticks, dtype=jnp.int32),
    )
    results = done[1]
    return (outputs[None], results[None])


def solution(mesh):
    placed = (
        P(None, "expert", None),
        P(None, "expert", None),
        P("section", None),
        P("section", None, "expert", None),
        P("section", None, "expert", None),
        P("section", "expert", None, None),
        P("section", "expert", None, None),
        P("section", "expert", None, None),
    )
    return jax.shard_map(
        local,
        mesh=mesh,
        in_specs=placed,
        out_specs=(P("section", None, "expert", None), P("section", None, "expert", None)),
        check_vma=False,
    )
```

profile of v0, /device:TPU:0, one launch (start us, length us, event | category | flops | bytes accessed | tf_op | source)
XLA Modules:
  0.0 1162.5 jit_solution(16980706059213436637)
XLA Ops:
  5.5 559.5 %while.33 = (s32[]{:T(128)}, bf16[32,4096]{1,0:T(8,128)(2,1)S(1)}, bf16[4,32,4096]{2,1,0:T(8,128)(2,1)}, bf16[4,32,4096]{2,1,0:T(8,128)(2,1)}, f32[4,8,9,768]{3,...) while((s32[]{:T(128)}, bf16[32,4096]{1,0:T(8,128)(2,1)S(1)}, ...), condition=%wide.region_8.9_spmd, body=%wide.region_0.8_spmd.sunk | while | flops 1380716800 | bytes 71540032 | solution.py:154
  12.2 7.3 all-to-all-start
  19.6 25.6 %all-to-all-done = bf16[8,9,4096]{2,1,0:T(8,128)(2,1)S(1)} async-done(((bf16[8,9,4096]{2,1,0:T(8,128)(2,1)}), bf16[8,9,4096]{2,1,0:T(8,128)(2,1)S(1)}, u32[]{:S(2)}, u32[]{:S(2)}) %all-to-all-start) | async-done | bytes 589856 | tf_op jit(solution)/shard_map/while/body/eval_jaxpr/all_to_all | solution.py:113
  45.2 11.0 conditional.4
  51.0 4.0 convolution_convert_fusion
  63.9 12.7 %all-to-all-done.1 = bf16[8,9,4096]{2,1,0:T(8,128)(2,1)S(1)} async-done(((bf16[8,9,4096]{2,1,0:T(8,128)(2,1)}), bf16[8,9,4096]{2,1,0:T(8,128)(2,1)S(1)}, u32[]{:S(2)}, u32[]{:S(2)}) %all-to-all-start.1) | async-done | bytes 589856 | tf_op jit(solution)/shard_map/while/body/eval_jaxpr/all_to_all | solution.py:73
  93.5 25.1 %all-to-all-done = bf16[8,9,4096]{2,1,0:T(8,128)(2,1)S(1)} async-done(((bf16[8,9,4096]{2,1,0:T(8,128)(2,1)}), bf16[8,9,4096]{2,1,0:T(8,128)(2,1)S(1)}, u32[]{:S(2)}, u32[]{:S(2)}) %all-to-all-start) | async-done | bytes 589856 | tf_op jit(solution)/shard_map/while/body/eval_jaxpr/all_to_all | solution.py:113
  118.6 11.0 conditional.4
  124.3 4.0 convolution_convert_fusion
  129.6 5.3 all-to-all-start.1
  139.0 22.4 %all-to-all-done.1 = bf16[8,9,4096]{2,1,0:T(8,128)(2,1)S(1)} async-done(((bf16[8,9,4096]{2,1,0:T(8,128)(2,1)}), bf16[8,9,4096]{2,1,0:T(8,128)(2,1)S(1)}, u32[]{:S(2)}, u32[]{:S(2)}) %all-to-all-start.1) | async-done | bytes 589856 | tf_op jit(solution)/shard_map/while/body/eval_jaxpr/all_to_all | solution.py:73
  174.5 4.2 all-to-all-start
  178.9 26.5 %all-to-all-done = bf16[8,9,4096]{2,1,0:T(8,128)(2,1)S(1)} async-done(((bf16[8,9,4096]{2,1,0:T(8,128)(2,1)}), bf16[8,9,4096]{2,1,0:T(8,128)(2,1)S(1)}, u32[]{:S(2)}, u32[]{:S(2)}) %all-to-all-start) | async-done | bytes 589856 | tf_op jit(solution)/shard_map/while/body/eval_jaxpr/all_to_all | solution.py:113
  205.5 11.0 conditional.4
  224.6 22.3 %all-to-all-done.1 = bf16[8,9,4096]{2,1,0:T(8,128)(2,1)S(1)} async-done(((bf16[8,9,4096]{2,1,0:T(8,128)(2,1)}), bf16[8,9,4096]{2,1,0:T(8,128)(2,1)S(1)}, u32[]{:S(2)}, u32[]{:S(2)}) %all-to-all-start.1) | async-done | bytes 589856 | tf_op jit(solution)/shard_map/while/body/eval_jaxpr/all_to_all | solution.py:73
  260.0 4.3 all-to-all-start
  264.4 26.5 %all-to-all-done = bf16[8,9,4096]{2,1,0:T(8,128)(2,1)S(1)} async-done(((bf16[8,9,4096]{2,1,0:T(8,128)(2,1)}), bf16[8,9,4096]{2,1,0:T(8,128)(2,1)S(1)}, u32[]{:S(2)}, u32[]{:S(2)}) %all-to-all-start) | async-done | bytes 589856 | tf_op jit(solution)/shard_map/while/body/eval_jaxpr/all_to_all | solution.py:113
  290.9 11.0 conditional.4
  302.0 4.1 all-to-all-start.1
  310.1 22.3 %all-to-all-done.1 = bf16[8,9,4096]{2,1,0:T(8,128)(2,1)S(1)} async-done(((bf16[8,9,4096]{2,1,0:T(8,128)(2,1)}), bf16[8,9,4096]{2,1,0:T(8,128)(2,1)S(1)}, u32[]{:S(2)}, u32[]{:S(2)}) %all-to-all-start.1) | async-done | bytes 589856 | tf_op jit(solution)/shard_map/while/body/eval_jaxpr/all_to_all | solution.py:73
  345.5 4.3 all-to-all-start
  349.9 26.5 %all-to-all-done = bf16[8,9,4096]{2,1,0:T(8,128)(2,1)S(1)} async-done(((bf16[8,9,4096]{2,1,0:T(8,128)(2,1)}), bf16[8,9,4096]{2,1,0:T(8,128)(2,1)S(1)}, u32[]{:S(2)}, u32[]{:S(2)}) %all-to-all-start) | async-done | bytes 589856 | tf_op jit(solution)/shard_map/while/body/eval_jaxpr/all_to_all | solution.py:113
  377.6 4.0 all-to-all-start.1
  385.7 19.7 %all-to-all-done.1 = bf16[8,9,4096]{2,1,0:T(8,128)(2,1)S(1)} async-done(((bf16[8,9,4096]{2,1,0:T(8,128)(2,1)}), bf16[8,9,4096]{2,1,0:T(8,128)(2,1)S(1)}, u32[]{:S(2)}, u32[]{:S(2)}) %all-to-all-start.1) | async-done | bytes 589856 | tf_op jit(solution)/shard_map/while/body/eval_jaxpr/all_to_all | solution.py:73
  409.4 5.6 collective-permute-start
  426.6 26.0 %all-to-all-done = bf16[8,9,4096]{2,1,0:T(8,128)(2,1)S(1)} async-done(((bf16[8,9,4096]{2,1,0:T(8,128)(2,1)}), bf16[8,9,4096]{2,1,0:T(8,128)(2,1)S(1)}, u32[]{:S(2)}, u32[]{:S(2)}) %all-to-all-start) | async-done | bytes 589856 | tf_op jit(solution)/shard_map/while/body/eval_jaxpr/all_to_all | solution.py:113
  453.7 4.4 all-to-all-start.1
  462.2 22.5 %all-to-all-done.1 = bf16[8,9,4096]{2,1,0:T(8,128)(2,1)S(1)} async-done(((bf16[8,9,4096]{2,1,0:T(8,128)(2,1)}), bf16[8,9,4096]{2,1,0:T(8,128)(2,1)S(1)}, u32[]{:S(2)}, u32[]{:S(2)}) %all-to-all-start.1) | async-done | bytes 589856 | tf_op jit(solution)/shard_map/while/body/eval_jaxpr/all_to_all | solution.py:73
  497.8 4.2 all-to-all-start
  502.2 23.6 %all-to-all-done = bf16[8,9,4096]{2,1,0:T(8,128)(2,1)S(1)} async-done(((bf16[8,9,4096]{2,1,0:T(8,128)(2,1)}), bf16[8,9,4096]{2,1,0:T(8,128)(2,1)S(1)}, u32[]{:S(2)}, u32[]{:S(2)}) %all-to-all-start) | async-done | bytes 589856 | tf_op jit(solution)/shard_map/while/body/eval_jaxpr/all_to_all | solution.py:113
  534.6 21.4 %all-to-all-done.1 = bf16[8,9,4096]{2,1,0:T(8,128)(2,1)S(1)} async-done(((bf16[8,9,4096]{2,1,0:T(8,128)(2,1)}), bf16[8,9,4096]{2,1,0:T(8,128)(2,1)S(1)}, u32[]{:S(2)}, u32[]{:S(2)}) %all-to-all-start.1) | async-done | bytes 589856 | tf_op jit(solution)/shard_map/while/body/eval_jaxpr/all_to_all | solution.py:73
  566.1 596.3 %while.34 = (s32[]{:T(128)}, bf16[32,4096]{1,0:T(8,128)(2,1)S(1)}, bf16[4,32,4096]{2,1,0:T(8,128)(2,1)}, pred[]{:T(512)}, s32[7]{0:T(128)S(1)}, /*index=5*/s32[]...) while((s32[]{:T(128)}, bf16[32,4096]{1,0:T(8,128)(2,1)S(1)}, ...), condition=%wide.region_17.18_spmd, body=%wide.region_9.17_spmd.sunk | while | flops 1401398400 | bytes 66230820 | solution.py:209
  574.5 23.7 %all-to-all-done.2 = bf16[8,9,4096]{2,1,0:T(8,128)(2,1)S(1)} async-done(((bf16[8,9,4096]{2,1,0:T(8,128)(2,1)}), bf16[8,9,4096]{2,1,0:T(8,128)(2,1)S(1)}, u32[]{:S(2)}, u32[]{:S(2)}) %all-to-all-start.2) | async-done | bytes 589856 | tf_op jit(solution)/shard_map/while/body/eval_jaxpr/all_to_all | solution.py:168
  604.5 24.3 %all-to-all-done.3 = bf16[8,9,4096]{2,1,0:T(8,128)(2,1)S(1)} async-done(((bf16[8,9,4096]{2,1,0:T(8,128)(2,1)}), bf16[8,9,4096]{2,1,0:T(8,128)(2,1)S(1)}, u32[]{:S(2)}, u32[]{:S(2)}) %all-to-all-start.3) | async-done | bytes 589856 | tf_op jit(solution)/shard_map/while/body/eval_jaxpr/all_to_all | solution.py:73
  648.2 25.2 %all-to-all-done.2 = bf16[8,9,4096]{2,1,0:T(8,128)(2,1)S(1)} async-done(((bf16[8,9,4096]{2,1,0:T(8,128)(2,1)}), bf16[8,9,4096]{2,1,0:T(8,128)(2,1)S(1)}, u32[]{:S(2)}, u32[]{:S(2)}) %all-to-all-start.2) | async-done | bytes 589856 | tf_op jit(solution)/shard_map/while/body/eval_jaxpr/all_to_all | solution.py:168
  674.5 4.2 all-to-all-start.3
  680.0 25.7 %all-to-all-done.3 = bf16[8,9,4096]{2,1,0:T(8,128)(2,1)S(1)} async-done(((bf16[8,9,4096]{2,1,0:T(8,128)(2,1)}), bf16[8,9,4096]{2,1,0:T(8,128)(2,1)S(1)}, u32[]{:S(2)}, u32[]{:S(2)}) %all-to-all-start.3) | async-done | bytes 589856 | tf_op jit(solution)/shard_map/while/body/eval_jaxpr/all_to_all | solution.py:73
  723.8 16.4 %all-to-all-done.2 = bf16[8,9,4096]{2,1,0:T(8,128)(2,1)S(1)} async-done(((bf16[8,9,4096]{2,1,0:T(8,128)(2,1)}), bf16[8,9,4096]{2,1,0:T(8,128)(2,1)S(1)}, u32[]{:S(2)}, u32[]{:S(2)}) %all-to-all-start.2) | async-done | bytes 589856 | tf_op jit(solution)/shard_map/while/body/eval_jaxpr/all_to_all | solution.py:168
  746.2 14.9 %all-to-all-done.3 = bf16[8,9,4096]{2,1,0:T(8,128)(2,1)S(1)} async-done(((bf16[8,9,4096]{2,1,0:T(8,128)(2,1)}), bf16[8,9,4096]{2,1,0:T(8,128)(2,1)S(1)}, u32[]{:S(2)}, u32[]{:S(2)}) %all-to-all-start.3) | async-done | bytes 589856 | tf_op jit(solution)/shard_map/while/body/eval_jaxpr/all_to_all | solution.py:73
  768.6 49.4 %collective-permute-done.1 = bf16[32,4096]{1,0:T(8,128)(2,1)S(1)} collective-permute-done((bf16[32,4096]{1,0:T(8,128)(2,1)S(1)}, bf16[32,4096]{1,0:T(8,128)(2,1)S(1)}, u32[]{:S(2)}, u32[]{:S(2)}) %collective-permute-start.1) | collective-permute-done | bytes 262176 | tf_op jit(solution)/shard_map/while/body/eval_jaxpr/ppermute | solution.py:12
  826.4 16.3 %all-to-all-done.2 = bf16[8,9,4096]{2,1,0:T(8,128)(2,1)S(1)} async-done(((bf16[8,9,4096]{2,1,0:T(8,128)(2,1)}), bf16[8,9,4096]{2,1,0:T(8,128)(2,1)S(1)}, u32[]{:S(2)}, u32[]{:S(2)}) %all-to-all-start.2) | async-done | bytes 589856 | tf_op jit(solution)/shard_map/while/body/eval_jaxpr/all_to_all | solution.py:168
  842.7 17.3 %conditional.5 = (bf16[8,9,4096]{2,1,0:T(8,128)(2,1)}) conditional(s32[]{:T(128)} %convert_element_type.173, () %tuple.92, (bf16[8,9,4096]{2,1,0:T(8,128)(2,1)S(1)}, bf16[768,4096]{1,0:T(8,128)(2,1)}, f32[4,8,9,768]{3,2,1,0:T(8,128)}, s32[]{:T(128)}, f32[4,8,9,768]{3,2,1,0:T(8,128)}, /*index=5*/bf16[4096,768]{1,0:T(8,128)(2,1)}, ...), branch_computations={%region_13.13_spmd, %region_14.14_spmd} | conditional | flops 1360429056 | bytes 47628376 | solution.py:178
  844.9 5.7 fusion.36
  851.7 5.0 fusion.5
  864.9 14.9 %all-to-all-done.3 = bf16[8,9,4096]{2,1,0:T(8,128)(2,1)S(1)} async-done(((bf16[8,9,4096]{2,1,0:T(8,128)(2,1)}), bf16[8,9,4096]{2,1,0:T(8,128)(2,1)S(1)}, u32[]{:S(2)}, u32[]{:S(2)}) %all-to-all-start.3) | async-done | bytes 589856 | tf_op jit(solution)/shard_map/while/body/eval_jaxpr/all_to_all | solution.py:73
  887.3 21.2 %collective-permute-done.1 = bf16[32,4096]{1,0:T(8,128)(2,1)S(1)} collective-permute-done((bf16[32,4096]{1,0:T(8,128)(2,1)S(1)}, bf16[32,4096]{1,0:T(8,128)(2,1)S(1)}, u32[]{:S(2)}, u32[]{:S(2)}) %collective-permute-start.1) | collective-permute-done | bytes 262176 | tf_op jit(solution)/shard_map/while/body/eval_jaxpr/ppermute | solution.py:12
  916.9 16.3 %all-to-all-done.2 = bf16[8,9,4096]{2,1,0:T(8,128)(2,1)S(1)} async-done(((bf16[8,9,4096]{2,1,0:T(8,128)(2,1)}), bf16[8,9,4096]{2,1,0:T(8,128)(2,1)S(1)}, u32[]{:S(2)}, u32[]{:S(2)}) %all-to-all-start.2) | async-done | bytes 589856 | tf_op jit(solution)/shard_map/while/body/eval_jaxpr/all_to_all | solution.py:168
  933.2 17.3 %conditional.5 = (bf16[8,9,4096]{2,1,0:T(8,128)(2,1)}) conditional(s32[]{:T(128)} %convert_element_type.173, () %tuple.92, (bf16[8,9,4096]{2,1,0:T(8,128)(2,1)S(1)}, bf16[768,4096]{1,0:T(8,128)(2,1)}, f32[4,8,9,768]{3,2,1,0:T(8,128)}, s32[]{:T(128)}, f32[4,8,9,768]{3,2,1,0:T(8,128)}, /*index=5*/bf16[4096,768]{1,0:T(8,128)(2,1)}, ...), branch_computations={%region_13.13_spmd, %region_14.14_spmd} | conditional | flops 1360429056 | bytes 47628376 | solution.py:178
  935.4 5.7 fusion.36
  942.1 5.0 fusion.5
  955.4 14.9 %all-to-all-done.3 = bf16[8,9,4096]{2,1,0:T(8,128)(2,1)S(1)} async-done(((bf16[8,9,4096]{2,1,0:T(8,128)(2,1)}), bf16[8,9,4096]{2,1,0:T(8,128)(2,1)S(1)}, u32[]{:S(2)}, u32[]{:S(2)}) %all-to-all-start.3) | async-done | bytes 589856 | tf_op jit(solution)/shard_map/while/body/eval_jaxpr/all_to_all | solution.py:73
  977.8 21.5 %collective-permute-done.1 = bf16[32,4096]{1,0:T(8,128)(2,1)S(1)} collective-permute-done((bf16[32,4096]{1,0:T(8,128)(2,1)S(1)}, bf16[32,4096]{1,0:T(8,128)(2,1)S(1)}, u32[]{:S(2)}, u32[]{:S(2)}) %collective-permute-start.1) | collective-permute-done | bytes 262176 | tf_op jit(solution)/shard_map/while/body/eval_jaxpr/ppermute | solution.py:12
  1007.7 16.3 %all-to-all-done.2 = bf16[8,9,4096]{2,1,0:T(8,128)(2,1)S(1)} async-done(((bf16[8,9,4096]{2,1,0:T(8,128)(2,1)}), bf16[8,9,4096]{2,1,0:T(8,128)(2,1)S(1)}, u32[]{:S(2)}, u32[]{:S(2)}) %all-to-all-start.2) | async-done | bytes 589856 | tf_op jit(solution)/shard_map/while/body/eval_jaxpr/all_to_all | solution.py:168
  1024.0 17.3 %conditional.5 = (bf16[8,9,4096]{2,1,0:T(8,128)(2,1)}) conditional(s32[]{:T(128)} %convert_element_type.173, () %tuple.92, (bf16[8,9,4096]{2,1,0:T(8,128)(2,1)S(1)}, bf16[768,4096]{1,0:T(8,128)(2,1)}, f32[4,8,9,768]{3,2,1,0:T(8,128)}, s32[]{:T(128)}, f32[4,8,9,768]{3,2,1,0:T(8,128)}, /*index=5*/bf16[4096,768]{1,0:T(8,128)(2,1)}, ...), branch_computations={%region_13.13_spmd, %region_14.14_spmd} | conditional | flops 1360429056 | bytes 47628376 | solution.py:178
  1026.3 5.7 fusion.36
  1033.0 5.0 fusion.5
  1046.3 15.2 %all-to-all-done.3 = bf16[8,9,4096]{2,1,0:T(8,128)(2,1)S(1)} async-done(((bf16[8,9,4096]{2,1,0:T(8,128)(2,1)}), bf16[8,9,4096]{2,1,0:T(8,128)(2,1)S(1)}, u32[]{:S(2)}, u32[]{:S(2)}) %all-to-all-start.3) | async-done | bytes 589856 | tf_op jit(solution)/shard_map/while/body/eval_jaxpr/all_to_all | solution.py:73
  1068.9 12.8 %collective-permute-done.1 = bf16[32,4096]{1,0:T(8,128)(2,1)S(1)} collective-permute-done((bf16[32,4096]{1,0:T(8,128)(2,1)S(1)}, bf16[32,4096]{1,0:T(8,128)(2,1)S(1)}, u32[]{:S(2)}, u32[]{:S(2)}) %collective-permute-start.1) | collective-permute-done | bytes 262176 | tf_op jit(solution)/shard_map/while/body/eval_jaxpr/ppermute | solution.py:12
  1090.1 24.6 %all-to-all-done.2 = bf16[8,9,4096]{2,1,0:T(8,128)(2,1)S(1)} async-done(((bf16[8,9,4096]{2,1,0:T(8,128)(2,1)}), bf16[8,9,4096]{2,1,0:T(8,128)(2,1)S(1)}, u32[]{:S(2)}, u32[]{:S(2)}) %all-to-all-start.2) | async-done | bytes 589856 | tf_op jit(solution)/shard_map/while/body/eval_jaxpr/all_to_all | solution.py:168
  1114.7 17.3 %conditional.5 = (bf16[8,9,4096]{2,1,0:T(8,128)(2,1)}) conditional(s32[]{:T(128)} %convert_element_type.173, () %tuple.92, (bf16[8,9,4096]{2,1,0:T(8,128)(2,1)S(1)}, bf16[768,4096]{1,0:T(8,128)(2,1)}, f32[4,8,9,768]{3,2,1,0:T(8,128)}, s32[]{:T(128)}, f32[4,8,9,768]{3,2,1,0:T(8,128)}, /*index=5*/bf16[4096,768]{1,0:T(8,128)(2,1)}, ...), branch_computations={%region_13.13_spmd, %region_14.14_spmd} | conditional | flops 1360429056 | bytes 47628376 | solution.py:178
  1117.0 5.7 fusion.36
  1123.7 5.0 fusion.5
  1132.0 4.5 all-to-all-start.3
  1137.9 15.0 %all-to-all-done.3 = bf16[8,9,4096]{2,1,0:T(8,128)(2,1)S(1)} async-done(((bf16[8,9,4096]{2,1,0:T(8,128)(2,1)}), bf16[8,9,4096]{2,1,0:T(8,128)(2,1)S(1)}, u32[]{:S(2)}, u32[]{:S(2)}) %all-to-all-start.3) | async-done | bytes 589856 | tf_op jit(solution)/shard_map/while/body/eval_jaxpr/all_to_all | solution.py:73
  (615 shorter events, 357.6 us)
Async XLA Ops:
  2.8 2.7 copy-start.5
  2.8 2.7 copy-start.6
  2.8 2.7 copy-start.7
  12.2 33.0 %all-to-all-start = ((bf16[8,9,4096]{2,1,0:T(8,128)(2,1)}), bf16[8,9,4096]{2,1,0:T(8,128)(2,1)S(1)}, u32[]{:S(2)}, u32[]{:S(2)}) async-start(bf16[8,9,4096]{2,1,0:T(8,128)(2,1)} %reshape.230), calls=%async_computation | async-start | bytes 2097152 | tf_op jit(solution)/shard_map/while/body/eval_jaxpr/all_to_all | solution.py:113
  45.2 4.6 copy-start
  56.2 20.4 %all-to-all-start.1 = ((bf16[8,9,4096]{2,1,0:T(8,128)(2,1)}), bf16[8,9,4096]{2,1,0:T(8,128)(2,1)S(1)}, u32[]{:S(2)}, u32[]{:S(2)}) async-start(bf16[8,9,4096]{2,1,0:T(8,128)(2,1)} %get-tuple-element.684), calls=%async_computation.1 | async-start | bytes 2097152 | tf_op jit(solution)/shard_map/while/body/eval_jaxpr/all_to_all | solution.py:73
  80.7 2.4 collective-permute-start
  89.7 28.8 %all-to-all-start = ((bf16[8,9,4096]{2,1,0:T(8,128)(2,1)}), bf16[8,9,4096]{2,1,0:T(8,128)(2,1)S(1)}, u32[]{:S(2)}, u32[]{:S(2)}) async-start(bf16[8,9,4096]{2,1,0:T(8,128)(2,1)} %reshape.230), calls=%async_computation | async-start | bytes 2097152 | tf_op jit(solution)/shard_map/while/body/eval_jaxpr/all_to_all | solution.py:113
  118.6 4.6 copy-start
  122.5 1.8 copy-start.1
  129.6 31.8 %all-to-all-start.1 = ((bf16[8,9,4096]{2,1,0:T(8,128)(2,1)}), bf16[8,9,4096]{2,1,0:T(8,128)(2,1)S(1)}, u32[]{:S(2)}, u32[]{:S(2)}) async-start(bf16[8,9,4096]{2,1,0:T(8,128)(2,1)} %get-tuple-element.684), calls=%async_computation.1 | async-start | bytes 2097152 | tf_op jit(solution)/shard_map/while/body/eval_jaxpr/all_to_all | solution.py:73
  165.4 2.5 collective-permute-start
  174.5 31.0 %all-to-all-start = ((bf16[8,9,4096]{2,1,0:T(8,128)(2,1)}), bf16[8,9,4096]{2,1,0:T(8,128)(2,1)S(1)}, u32[]{:S(2)}, u32[]{:S(2)}) async-start(bf16[8,9,4096]{2,1,0:T(8,128)(2,1)} %reshape.230), calls=%async_computation | async-start | bytes 2097152 | tf_op jit(solution)/shard_map/while/body/eval_jaxpr/all_to_all | solution.py:113
  205.5 4.6 copy-start
  209.4 1.8 copy-start.1
  216.5 30.4 %all-to-all-start.1 = ((bf16[8,9,4096]{2,1,0:T(8,128)(2,1)}), bf16[8,9,4096]{2,1,0:T(8,128)(2,1)S(1)}, u32[]{:S(2)}, u32[]{:S(2)}) async-start(bf16[8,9,4096]{2,1,0:T(8,128)(2,1)} %get-tuple-element.684), calls=%async_computation.1 | async-start | bytes 2097152 | tf_op jit(solution)/shard_map/while/body/eval_jaxpr/all_to_all | solution.py:73
  251.0 2.4 collective-permute-start
  260.0 30.9 %all-to-all-start = ((bf16[8,9,4096]{2,1,0:T(8,128)(2,1)}), bf16[8,9,4096]{2,1,0:T(8,128)(2,1)S(1)}, u32[]{:S(2)}, u32[]{:S(2)}) async-start(bf16[8,9,4096]{2,1,0:T(8,128)(2,1)} %reshape.230), calls=%async_computation | async-start | bytes 2097152 | tf_op jit(solution)/shard_map/while/body/eval_jaxpr/all_to_all | solution.py:113
  290.9 4.6 copy-start
  294.9 1.8 copy-start.1
  302.0 30.4 %all-to-all-start.1 = ((bf16[8,9,4096]{2,1,0:T(8,128)(2,1)}), bf16[8,9,4096]{2,1,0:T(8,128)(2,1)S(1)}, u32[]{:S(2)}, u32[]{:S(2)}) async-start(bf16[8,9,4096]{2,1,0:T(8,128)(2,1)} %get-tuple-element.684), calls=%async_computation.1 | async-start | bytes 2097152 | tf_op jit(solution)/shard_map/while/body/eval_jaxpr/all_to_all | solution.py:73
  336.5 2.4 collective-permute-start
  345.5 31.0 %all-to-all-start = ((bf16[8,9,4096]{2,1,0:T(8,128)(2,1)}), bf16[8,9,4096]{2,1,0:T(8,128)(2,1)S(1)}, u32[]{:S(2)}, u32[]{:S(2)}) async-start(bf16[8,9,4096]{2,1,0:T(8,128)(2,1)} %reshape.230), calls=%async_computation | async-start | bytes 2097152 | tf_op jit(solution)/shard_map/while/body/eval_jaxpr/all_to_all | solution.py:113
  377.6 27.8 %all-to-all-start.1 = ((bf16[8,9,4096]{2,1,0:T(8,128)(2,1)}), bf16[8,9,4096]{2,1,0:T(8,128)(2,1)S(1)}, u32[]{:S(2)}, u32[]{:S(2)}) async-start(bf16[8,9,4096]{2,1,0:T(8,128)(2,1)} %get-tuple-element.684), calls=%async_computation.1 | async-start | bytes 2097152 | tf_op jit(solution)/shard_map/while/body/eval_jaxpr/all_to_all | solution.py:73
  409.4 6.8 collective-permute-start
  422.8 29.8 %all-to-all-start = ((bf16[8,9,4096]{2,1,0:T(8,128)(2,1)}), bf16[8,9,4096]{2,1,0:T(8,128)(2,1)S(1)}, u32[]{:S(2)}, u32[]{:S(2)}) async-start(bf16[8,9,4096]{2,1,0:T(8,128)(2,1)} %reshape.230), calls=%async_computation | async-start | bytes 2097152 | tf_op jit(solution)/shard_map/while/body/eval_jaxpr/all_to_all | solution.py:113
  453.7 30.9 %all-to-all-start.1 = ((bf16[8,9,4096]{2,1,0:T(8,128)(2,1)}), bf16[8,9,4096]{2,1,0:T(8,128)(2,1)S(1)}, u32[]{:S(2)}, u32[]{:S(2)}) async-start(bf16[8,9,4096]{2,1,0:T(8,128)(2,1)} %get-tuple-element.684), calls=%async_computation.1 | async-start | bytes 2097152 | tf_op jit(solution)/shard_map/while/body/eval_jaxpr/all_to_all | solution.py:73
  488.7 2.6 collective-permute-start
  497.8 27.9 %all-to-all-start = ((bf16[8,9,4096]{2,1,0:T(8,128)(2,1)}), bf16[8,9,4096]{2,1,0:T(8,128)(2,1)S(1)}, u32[]{:S(2)}, u32[]{:S(2)}) async-start(bf16[8,9,4096]{2,1,0:T(8,128)(2,1)} %reshape.230), calls=%async_computation | async-start | bytes 2097152 | tf_op jit(solution)/shard_map/while/body/eval_jaxpr/all_to_all | solution.py:113
  526.9 29.0 %all-to-all-start.1 = ((bf16[8,9,4096]{2,1,0:T(8,128)(2,1)}), bf16[8,9,4096]{2,1,0:T(8,128)(2,1)S(1)}, u32[]{:S(2)}, u32[]{:S(2)}) async-start(bf16[8,9,4096]{2,1,0:T(8,128)(2,1)} %get-tuple-element.684), calls=%async_computation.1 | async-start | bytes 2097152 | tf_op jit(solution)/shard_map/while/body/eval_jaxpr/all_to_all | solution.py:73
  560.0 5.1 collective-permute-start
  571.0 27.2 %all-to-all-start.2 = ((bf16[8,9,4096]{2,1,0:T(8,128)(2,1)}), bf16[8,9,4096]{2,1,0:T(8,128)(2,1)S(1)}, u32[]{:S(2)}, u32[]{:S(2)}) async-start(bf16[8,9,4096]{2,1,0:T(8,128)(2,1)} %reshape.236), calls=%async_computation.2 | async-start | bytes 2097152 | tf_op jit(solution)/shard_map/while/body/eval_jaxpr/all_to_all | solution.py:168
  599.3 29.6 %all-to-all-start.3 = ((bf16[8,9,4096]{2,1,0:T(8,128)(2,1)}), bf16[8,9,4096]{2,1,0:T(8,128)(2,1)S(1)}, u32[]{:S(2)}, u32[]{:S(2)}) async-start(bf16[8,9,4096]{2,1,0:T(8,128)(2,1)} %get-tuple-element.844), calls=%async_computation.3 | async-start | bytes 2097152 | tf_op jit(solution)/shard_map/while/body/eval_jaxpr/all_to_all | solution.py:73
  635.0 4.7 collective-permute-start.1
  644.5 28.9 %all-to-all-start.2 = ((bf16[8,9,4096]{2,1,0:T(8,128)(2,1)}), bf16[8,9,4096]{2,1,0:T(8,128)(2,1)S(1)}, u32[]{:S(2)}, u32[]{:S(2)}) async-start(bf16[8,9,4096]{2,1,0:T(8,128)(2,1)} %reshape.236), calls=%async_computation.2 | async-start | bytes 2097152 | tf_op jit(solution)/shard_map/while/body/eval_jaxpr/all_to_all | solution.py:168
  674.5 31.2 %all-to-all-start.3 = ((bf16[8,9,4096]{2,1,0:T(8,128)(2,1)}), bf16[8,9,4096]{2,1,0:T(8,128)(2,1)S(1)}, u32[]{:S(2)}, u32[]{:S(2)}) async-start(bf16[8,9,4096]{2,1,0:T(8,128)(2,1)} %get-tuple-element.844), calls=%async_computation.3 | async-start | bytes 2097152 | tf_op jit(solution)/shard_map/while/body/eval_jaxpr/all_to_all | solution.py:73
  711.9 3.4 collective-permute-start.1
  720.1 20.1 %all-to-all-start.2 = ((bf16[8,9,4096]{2,1,0:T(8,128)(2,1)}), bf16[8,9,4096]{2,1,0:T(8,128)(2,1)S(1)}, u32[]{:S(2)}, u32[]{:S(2)}) async-start(bf16[8,9,4096]{2,1,0:T(8,128)(2,1)} %reshape.236), calls=%async_computation.2 | async-start | bytes 2097152 | tf_op jit(solution)/shard_map/while/body/eval_jaxpr/all_to_all | solution.py:168
  741.2 19.9 %all-to-all-start.3 = ((bf16[8,9,4096]{2,1,0:T(8,128)(2,1)}), bf16[8,9,4096]{2,1,0:T(8,128)(2,1)S(1)}, u32[]{:S(2)}, u32[]{:S(2)}) async-start(bf16[8,9,4096]{2,1,0:T(8,128)(2,1)} %get-tuple-element.844), calls=%async_computation.3 | async-start | bytes 2097152 | tf_op jit(solution)/shard_map/while/body/eval_jaxpr/all_to_all | solution.py:73
  767.3 50.7 %collective-permute-start.1 = (bf16[32,4096]{1,0:T(8,128)(2,1)S(1)}, bf16[32,4096]{1,0:T(8,128)(2,1)S(1)}, u32[]{:S(2)}, u32[]{:S(2)}) collective-permute-start(bf16[32,4096]{1,0:T(8,128)(2,1)S(1)} %get-tuple-element.713), channel_id=1, source_target_pairs={{8,0},{16,8},{24,16},{9,1},{17,9},{25,17},{10,2},{18,10},{26,18},{... | collective-permute-start | bytes 786440 | tf_op jit(solution)/shard_map/while/body/eval_jaxpr/ppermute | solution.py:12
  822.8 19.9 %all-to-all-start.2 = ((bf16[8,9,4096]{2,1,0:T(8,128)(2,1)}), bf16[8,9,4096]{2,1,0:T(8,128)(2,1)S(1)}, u32[]{:S(2)}, u32[]{:S(2)}) async-start(bf16[8,9,4096]{2,1,0:T(8,128)(2,1)} %reshape.236), calls=%async_computation.2 | async-start | bytes 2097152 | tf_op jit(solution)/shard_map/while/body/eval_jaxpr/all_to_all | solution.py:168
  844.9 11.8 %slice-start = ((s8[6291456]{0:T(1024)(128)(4,1)}), s8[2097152]{0:T(1024)(128)(4,1)S(1)}, s32[]{:S(2)}) async-start(s8[6291456]{0:T(1024)(128)(4,1)} %bitcast.152), calls=%async_computation.4 | async-start | bytes 4194304 | tf_op jit(solution)/shard_map/while/body/eval_jaxpr/cond
  851.6 5.1 slice-start.1
  851.6 5.1 copy-start.3
  860.0 19.9 %all-to-all-start.3 = ((bf16[8,9,4096]{2,1,0:T(8,128)(2,1)}), bf16[8,9,4096]{2,1,0:T(8,128)(2,1)S(1)}, u32[]{:S(2)}, u32[]{:S(2)}) async-start(bf16[8,9,4096]{2,1,0:T(8,128)(2,1)} %get-tuple-element.844), calls=%async_computation.3 | async-start | bytes 2097152 | tf_op jit(solution)/shard_map/while/body/eval_jaxpr/all_to_all | solution.py:73
  886.0 22.5 %collective-permute-start.1 = (bf16[32,4096]{1,0:T(8,128)(2,1)S(1)}, bf16[32,4096]{1,0:T(8,128)(2,1)S(1)}, u32[]{:S(2)}, u32[]{:S(2)}) collective-permute-start(bf16[32,4096]{1,0:T(8,128)(2,1)S(1)} %get-tuple-element.713), channel_id=1, source_target_pairs={{8,0},{16,8},{24,16},{9,1},{17,9},{25,17},{10,2},{18,10},{26,18},{... | collective-permute-start | bytes 786440 | tf_op jit(solution)/shard_map/while/body/eval_jaxpr/ppermute | solution.py:12
  913.3 19.9 %all-to-all-start.2 = ((bf16[8,9,4096]{2,1,0:T(8,128)(2,1)}), bf16[8,9,4096]{2,1,0:T(8,128)(2,1)S(1)}, u32[]{:S(2)}, u32[]{:S(2)}) async-start(bf16[8,9,4096]{2,1,0:T(8,128)(2,1)} %reshape.236), calls=%async_computation.2 | async-start | bytes 2097152 | tf_op jit(solution)/shard_map/while/body/eval_jaxpr/all_to_all | solution.py:168
  935.4 11.8 %slice-start = ((s8[6291456]{0:T(1024)(128)(4,1)}), s8[2097152]{0:T(1024)(128)(4,1)S(1)}, s32[]{:S(2)}) async-start(s8[6291456]{0:T(1024)(128)(4,1)} %bitcast.152), calls=%async_computation.4 | async-start | bytes 4194304 | tf_op jit(solution)/shard_map/while/body/eval_jaxpr/cond
  942.1 5.1 slice-start.1
  942.1 5.1 copy-start.3
  950.5 19.9 %all-to-all-start.3 = ((bf16[8,9,4096]{2,1,0:T(8,128)(2,1)}), bf16[8,9,4096]{2,1,0:T(8,128)(2,1)S(1)}, u32[]{:S(2)}, u32[]{:S(2)}) async-start(bf16[8,9,4096]{2,1,0:T(8,128)(2,1)} %get-tuple-element.844), calls=%async_computation.3 | async-start | bytes 2097152 | tf_op jit(solution)/shard_map/while/body/eval_jaxpr/all_to_all | solution.py:73
  976.5 22.8 %collective-permute-start.1 = (bf16[32,4096]{1,0:T(8,128)(2,1)S(1)}, bf16[32,4096]{1,0:T(8,128)(2,1)S(1)}, u32[]{:S(2)}, u32[]{:S(2)}) collective-permute-start(bf16[32,4096]{1,0:T(8,128)(2,1)S(1)} %get-tuple-element.713), channel_id=1, source_target_pairs={{8,0},{16,8},{24,16},{9,1},{17,9},{25,17},{10,2},{18,10},{26,18},{... | collective-permute-start | bytes 786440 | tf_op jit(solution)/shard_map/while/body/eval_jaxpr/ppermute | solution.py:12
  1004.1 19.9 %all-to-all-start.2 = ((bf16[8,9,4096]{2,1,0:T(8,128)(2,1)}), bf16[8,9,4096]{2,1,0:T(8,128)(2,1)S(1)}, u32[]{:S(2)}, u32[]{:S(2)}) async-start(bf16[8,9,4096]{2,1,0:T(8,128)(2,1)} %reshape.236), calls=%async_computation.2 | async-start | bytes 2097152 | tf_op jit(solution)/shard_map/while/body/eval_jaxpr/all_to_all | solution.py:168
  1026.3 11.8 %slice-start = ((s8[6291456]{0:T(1024)(128)(4,1)}), s8[2097152]{0:T(1024)(128)(4,1)S(1)}, s32[]{:S(2)}) async-start(s8[6291456]{0:T(1024)(128)(4,1)} %bitcast.152), calls=%async_computation.4 | async-start | bytes 4194304 | tf_op jit(solution)/shard_map/while/body/eval_jaxpr/cond
  1033.0 5.1 slice-start.1
  1033.0 5.1 copy-start.3
  1041.3 20.2 %all-to-all-start.3 = ((bf16[8,9,4096]{2,1,0:T(8,128)(2,1)}), bf16[8,9,4096]{2,1,0:T(8,128)(2,1)S(1)}, u32[]{:S(2)}, u32[]{:S(2)}) async-start(bf16[8,9,4096]{2,1,0:T(8,128)(2,1)} %get-tuple-element.844), calls=%async_computation.3 | async-start | bytes 2097152 | tf_op jit(solution)/shard_map/while/body/eval_jaxpr/all_to_all | solution.py:73
  1067.6 14.1 %collective-permute-start.1 = (bf16[32,4096]{1,0:T(8,128)(2,1)S(1)}, bf16[32,4096]{1,0:T(8,128)(2,1)S(1)}, u32[]{:S(2)}, u32[]{:S(2)}) collective-permute-start(bf16[32,4096]{1,0:T(8,128)(2,1)S(1)} %get-tuple-element.713), channel_id=1, source_target_pairs={{8,0},{16,8},{24,16},{9,1},{17,9},{25,17},{10,2},{18,10},{26,18},{... | collective-permute-start | bytes 786440 | tf_op jit(solution)/shard_map/while/body/eval_jaxpr/ppermute | solution.py:12
  1086.5 28.2 %all-to-all-start.2 = ((bf16[8,9,4096]{2,1,0:T(8,128)(2,1)}), bf16[8,9,4096]{2,1,0:T(8,128)(2,1)S(1)}, u32[]{:S(2)}, u32[]{:S(2)}) async-start(bf16[8,9,4096]{2,1,0:T(8,128)(2,1)} %reshape.236), calls=%async_computation.2 | async-start | bytes 2097152 | tf_op jit(solution)/shard_map/while/body/eval_jaxpr/all_to_all | solution.py:168
  1117.0 11.8 %slice-start = ((s8[6291456]{0:T(1024)(128)(4,1)}), s8[2097152]{0:T(1024)(128)(4,1)S(1)}, s32[]{:S(2)}) async-start(s8[6291456]{0:T(1024)(128)(4,1)} %bitcast.152), calls=%async_computation.4 | async-start | bytes 4194304 | tf_op jit(solution)/shard_map/while/body/eval_jaxpr/cond
  1123.7 5.1 slice-start.1
  1123.7 5.1 copy-start.3
  1132.0 20.9 %all-to-all-start.3 = ((bf16[8,9,4096]{2,1,0:T(8,128)(2,1)}), bf16[8,9,4096]{2,1,0:T(8,128)(2,1)S(1)}, u32[]{:S(2)}, u32[]{:S(2)}) async-start(bf16[8,9,4096]{2,1,0:T(8,128)(2,1)} %get-tuple-element.844), calls=%async_computation.3 | async-start | bytes 2097152 | tf_op jit(solution)/shard_map/while/body/eval_jaxpr/all_to_all | solution.py:73
  1159.1 3.4 collective-permute-start.1
  (12 other events, 16.7 us)
where the time goes:
time: 1170 us; the launch traced here: 1160 us
  waiting for transfers between devices  700 us (60%)
  local copies, waits for them, and re-layouts  140 us (12%)
  starting transfers between devices  138 us (12%)
  matrix products  92.5 us (8%)
  other arithmetic  79.3 us (7%)
  loops' own time  11.9 us (1%)
    all_to_all x14, waiting for transfers between devices, return_rows(): lax.all_to_all(rows, 'expert', split_axis=0, concat_axis=0, tiled=True)  268 us
    all_to_all x7, waiting for transfers between devices, forward_work(): lax.all_to_all(send, 'expert', split_axis=0, concat_axis=0, tiled=True)  180 us
    all_to_all x7, waiting for transfers between devices, backward_work(): lax.all_to_all(grad_send, 'expert', split_axis=0, concat_axis=0, tiled=True)  139 us
    ppermute x14, waiting for transfers between devices, passed_along(): lax.ppermute(value, axis, [(source, source + steps) for source in range(l...  114 us
    all_to_all x14, starting transfers between devices, return_rows(): lax.all_to_all(rows, 'expert', split_axis=0, concat_axis=0, tiled=True)  55.8 us
    dot_general x12, matrix products, contract_last(): lax.dot_general(left, right, (((1,), (1,)), ((), ())), preferred_element_...  50.9 us
    all_to_all x7, starting transfers between devices, forward_work(): lax.all_to_all(send, 'expert', split_axis=0, concat_axis=0, tiled=True)  31.3 us
    all_to_all x7, starting transfers between devices, backward_work(): lax.all_to_all(grad_send, 'expert', split_axis=0, concat_axis=0, tiled=True)  25.2 us
  transfers between devices with their start and end apart: 42, of which 42 were waited for; matrix products, arithmetic and copies ran while one was open for 4% of the time, Pallas kernels for 0%

commit v1 on v0

v1 whole, which is shorter than its diff:
```python
import functools

import jax
import jax.numpy as jnp
from jax import lax
from jax.experimental import pallas as pl
from jax.experimental.pallas import tpu as pltpu
from jax.sharding import PartitionSpec as P

EPS = 1e-06
MESH = pl.DeviceIdType.MESH
PIECE = 256
FOLD = 16
F32 = jnp.float32
BF16 = jnp.bfloat16


def mm(left, right):
    return jnp.dot(left, right, preferred_element_type=F32)


def mm_last(left, right):
    return lax.dot_general(left, right, (((1,), (1,)), ((), ())), preferred_element_type=F32)


def onehot(condition):
    return jnp.where(condition, 1.0, 0.0).astype(F32)


def kernel(
    experts, sections, capacity,
    inputs, cotangent, gain, route, route_t, gate, w_gate, w_up, w_down,
    hidden, grads,
    wg, wu, wd, xin, dyin, sent, got, kept_gate, kept_up, wide, narrow, inner_a, inner_b,
    weight_sem, send_sem, recv_sem, pass_send, pass_recv,
):
    micro, tok, width = inputs.shape
    inner = wg.shape[1]
    rows = experts * capacity
    block = capacity * FOLD
    pieces = width // PIECE
    section = lax.axis_index("section")
    me = lax.axis_index("expert")

    weight_copies = [
        pltpu.make_async_copy(source, target, weight_sem.at[i])
        for i, (source, target) in enumerate(((w_gate, wg), (w_up, wu), (w_down, wd)))
    ]
    for copy in weight_copies:
        copy.start()

    barrier = pltpu.get_barrier_semaphore()
    for d in range(1, experts):
        pl.semaphore_signal(
            barrier, inc=1, device_id={"expert": lax.rem(me + d, experts)}, device_id_type=MESH
        )
    for d in (1, sections - 1):
        pl.semaphore_signal(
            barrier, inc=1, device_id={"section": lax.rem(section + d, sections)},
            device_id_type=MESH,
        )

    @pl.when(section == 0)
    def _():
        xin[...] = inputs[...]

    @pl.when(section == sections - 1)
    def _():
        dyin[...] = cotangent[...]

    pl.semaphore_wait(barrier, experts + 1)

    def part(e):
        return pl.ds(pl.multiple_of(e * block, 16), block)

    def exchange(kind, m, peer):
        return pltpu.make_async_remote_copy(
            src_ref=sent.at[kind, m, part(peer)],
            dst_ref=got.at[kind, m, part(me)],
            send_sem=send_sem.at[kind, m, peer],
            recv_sem=recv_sem.at[kind, m, me],
            device_id={"expert": peer},
            device_id_type=MESH,
        )

    def arrival(kind, m, peer):
        return pltpu.make_async_remote_copy(
            src_ref=sent.at[kind, m, part(me)],
            dst_ref=got.at[kind, m, part(peer)],
            send_sem=send_sem.at[kind, m, me],
            recv_sem=recv_sem.at[kind, m, peer],
            device_id={"expert": peer},
            device_id_type=MESH,
        )

    def ship(kind, m):
        for d in range(1, experts):
            exchange(kind, m, lax.rem(me + d, experts)).start()
        got[kind, m, part(me), :] = sent[kind, m, part(me), :]

    def collect(kind, m):
        for d in range(1, experts):
            arrival(kind, m, lax.rem(me + d, experts)).wait_recv()

    def hidden_pass(m):
        return pltpu.make_async_remote_copy(
            src_ref=hidden.at[m], dst_ref=xin.at[m],
            send_sem=pass_send.at[0, m], recv_sem=pass_recv.at[0, m],
            device_id={"section": lax.rem(section + 1, sections)}, device_id_type=MESH,
        )

    def grads_pass(m):
        return pltpu.make_async_remote_copy(
            src_ref=grads.at[m], dst_ref=dyin.at[m],
            send_sem=pass_send.at[1, m], recv_sem=pass_recv.at[1, m],
            device_id={"section": lax.rem(section + sections - 1, sections)},
            device_id_type=MESH,
        )

    span = 8 * FOLD
    row_i = lax.broadcasted_iota(jnp.int32, (span, span), 0)
    col_i = lax.broadcasted_iota(jnp.int32, (span, span), 1)

    def fold(kind, m):
        order = onehot(col_i == (row_i % FOLD) * 8 + row_i // FOLD).astype(BF16)

        def step(g, _):
            at = pl.ds(pl.multiple_of(g * 8, 8), 8)
            stack = jnp.concatenate(
                [wide[at, p * PIECE:(p + 1) * PIECE] for p in range(pieces)], axis=0
            ).astype(BF16)
            sent[kind, m, pl.ds(pl.multiple_of(g * span, span), span), :] = mm(
                order, stack
            ).astype(BF16)
            return 0

        lax.fori_loop(0, rows // 8, step, 0, unroll=True)

    def unfold(kind, m):
        order = onehot(col_i == (row_i % 8) * FOLD + row_i // 8).astype(BF16)

        def step(g, _):
            at = pl.ds(pl.multiple_of(g * 8, 8), 8)
            flat = mm(order, got[kind, m, pl.ds(pl.multiple_of(g * span, span), span), :])
            for p in range(pieces):
                wide[at, p * PIECE:(p + 1) * PIECE] = flat[p * 8:(p + 1) * 8]
            return 0

        lax.fori_loop(0, rows // 8, step, 0, unroll=True)
        narrow[...] = wide[...].astype(BF16)

    def tables_t(m):
        expert = lax.broadcasted_iota(jnp.int32, (experts, tok), 0)
        names = route_t[m]
        ohs = [onehot(names[k:k + 1] == expert) for k in range(2)]
        earlier = onehot(
            lax.broadcasted_iota(jnp.int32, (tok, tok), 0)
            < lax.broadcasted_iota(jnp.int32, (tok, tok), 1)
        )
        before = mm((ohs[0] + ohs[1]).astype(BF16), earlier.astype(BF16))
        slot = lax.broadcasted_iota(jnp.int32, (rows, tok), 0).astype(F32)
        out = []
        for k in range(2):
            place = names[k:k + 1].astype(F32) * capacity + jnp.sum(
                ohs[k] * before, axis=0, keepdims=True
            )
            out.append(onehot(slot == place))
        return out

    def tables(m):
        expert = lax.broadcasted_iota(jnp.int32, (tok, experts), 1)
        names = route[m]
        ohs = [onehot(names[:, k:k + 1] == expert) for k in range(2)]
        earlier = onehot(
            lax.broadcasted_iota(jnp.int32, (tok, tok), 1)
            < lax.broadcasted_iota(jnp.int32, (tok, tok), 0)
        )
        before = mm(earlier.astype(BF16), (ohs[0] + ohs[1]).astype(BF16))
        slot = lax.broadcasted_iota(jnp.int32, (tok, rows), 1).astype(F32)
        out = []
        for k in range(2):
            place = names[:, k:k + 1].astype(F32) * capacity + jnp.sum(
                ohs[k] * before, axis=1, keepdims=True
            )
            out.append(onehot(slot == place))
        return out

    def rms_of(values):
        return lax.rsqrt(jnp.mean(values * values, axis=-1, keepdims=True) + EPS)

    def forward_send(m):
        @pl.when(section > 0)
        def _():
            hidden_pass(m).wait_recv()

        values = xin[m].astype(F32)
        normed = (values * rms_of(values) * gain[...]).astype(BF16)
        first, second = tables_t(m)
        wide[...] = mm((first + second).astype(BF16), normed)
        fold(0, m)
        ship(0, m)

    def forward_expert(m):
        @pl.when(m == 0)
        def _():
            for copy in weight_copies:
                copy.wait()

        collect(0, m)
        unfold(0, m)

        def up(n, _):
            at = pl.ds(pl.multiple_of(n * 256, 256), 256)
            pre_gate = mm(narrow[...], wg[:, at])
            pre_up = mm(narrow[...], wu[:, at])
            kept_gate[m, :, at] = pre_gate
            kept_up[m, :, at] = pre_up
            inner_a[:, at] = (pre_gate * jax.nn.sigmoid(pre_gate) * pre_up).astype(BF16)
            return 0

        lax.fori_loop(0, inner // 256, up, 0)

        def down(n, _):
            at = pl.ds(pl.multiple_of(n * 512, 512), 512)
            wide[:, at] = mm(inner_a[...], wd[:, at])
            return 0

        lax.fori_loop(0, width // 512, down, 0)
        fold(1, m)
        ship(1, m)

    def forward_merge(m):
        collect(1, m)
        unfold(1, m)
        first, second = tables(m)
        weights = gate[m]
        mixed = (
            xin[m].astype(F32)
            + weights[:, 0:1] * mm(first.astype(BF16), narrow[...])
            + weights[:, 1:2] * mm(second.astype(BF16), narrow[...])
        )
        hidden[m] = mixed.astype(BF16)

        @pl.when(section < sections - 1)
        def _():
            hidden_pass(m).start()

    def backward_send(m):
        @pl.when(section < sections - 1)
        def _():
            grads_pass(m).wait_recv()

        grad_out = dyin[m].astype(F32)
        weights = gate[m]
        scaled = jnp.concatenate(
            [(weights[:, k:k + 1] * grad_out).astype(BF16) for k in range(2)], axis=0
        )
        table = jnp.concatenate(tables_t(m), axis=1).astype(BF16)
        wide[...] = mm(table, scaled)
        fold(2, m)
        ship(2, m)

    def backward_expert(m):
        collect(2, m)
        unfold(2, m)

        def down(n, _):
            at = pl.ds(pl.multiple_of(n * 256, 256), 256)
            d_hidden = mm_last(narrow[...], wd[at, :])
            pre_gate = kept_gate[m, :, at]
            pre_up = kept_up[m, :, at]
            sigma = jax.nn.sigmoid(pre_gate)
            inner_a[:, at] = (
                d_hidden * pre_up * sigma * (1.0 + pre_gate * (1.0 - sigma))
            ).astype(BF16)
            inner_b[:, at] = (d_hidden * pre_gate * sigma).astype(BF16)
            return 0

        lax.fori_loop(0, inner // 256, down, 0)

        def up(n, _):
            at = pl.ds(pl.multiple_of(n * 512, 512), 512)
            wide[:, at] = mm_last(inner_a[...], wg[at, :]) + mm_last(inner_b[...], wu[at, :])
            return 0

        lax.fori_loop(0, width // 512, up, 0)
        fold(3, m)
        ship(3, m)

    def backward_merge(m):
        collect(3, m)
        unfold(3, m)
        first, second = tables(m)
        values = xin[m].astype(F32)
        scale = rms_of(values)
        weighted = mm((first + second).astype(BF16), narrow[...]) * gain[...]
        result = (
            dyin[m].astype(F32)
            + scale * weighted
            - values
            * (scale * scale * scale)
            * jnp.mean(values * weighted, axis=-1, keepdims=True)
        )
        grads[m] = result.astype(BF16)

        @pl.when(section > 0)
        def _():
            grads_pass(m).start()

    def tick(t, _):
        ahead = t - section
        back = t - (2 * sections - 2 - section)

        def guarded(stage, m):
            @pl.when((m >= 0) & (m < micro))
            def _():
                stage(m)

        guarded(forward_send, ahead)
        guarded(backward_send, back)
        guarded(forward_expert, ahead)
        guarded(backward_expert, back)
        guarded(forward_merge, ahead)
        guarded(backward_merge, back)
        return 0

    lax.fori_loop(0, 2 * sections + micro - 2, tick, 0)

    def drain(m, _):
        for kind in range(4):
            for d in range(1, experts):
                exchange(kind, m, lax.rem(me + d, experts)).wait_send()

        @pl.when(section < sections - 1)
        def _():
            hidden_pass(m).wait_send()

        @pl.when(section > 0)
        def _():
            grads_pass(m).wait_send()

        return 0

    lax.fori_loop(0, micro, drain, 0)


def local(inputs, cotangent, gain, route, gate, w_gate, w_up, w_down):
    micro, tok, width = inputs.shape
    top = route.shape[-1]
    experts = lax.axis_size("expert")
    sections = lax.axis_size("section")
    capacity = tok * top * 7 // (6 * experts)
    rows = experts * capacity
    inner = w_gate.shape[-1]
    vmem = pl.BlockSpec(memory_space=pltpu.VMEM)
    hbm = pl.BlockSpec(memory_space=pl.ANY)
    shape = jax.ShapeDtypeStruct((micro, tok, width), BF16)
    hidden, grads = pl.pallas_call(
        functools.partial(kernel, experts, sections, capacity),
        out_shape=(shape, shape),
        in_specs=[vmem] * 6 + [hbm] * 3,
        out_specs=(vmem, vmem),
        scratch_shapes=[
            pltpu.VMEM((width, inner), BF16),
            pltpu.VMEM((width, inner), BF16),
            pltpu.VMEM((inner, width), BF16),
            pltpu.VMEM((micro, tok, width), BF16),
            pltpu.VMEM((micro, tok, width), BF16),
            pltpu.VMEM((4, micro, rows * FOLD, PIECE), BF16),
            pltpu.VMEM((4, micro, rows * FOLD, PIECE), BF16),
            pltpu.VMEM((micro, rows, inner), F32),
            pltpu.VMEM((micro, rows, inner), F32),
            pltpu.VMEM((rows, width), F32),
            pltpu.VMEM((rows, width), BF16),
            pltpu.VMEM((rows, inner), BF16),
            pltpu.VMEM((rows, inner), BF16),
            pltpu.SemaphoreType.DMA((3,)),
            pltpu.SemaphoreType.DMA((4, micro, experts)),
            pltpu.SemaphoreType.DMA((4, micro, experts)),
            pltpu.SemaphoreType.DMA((2, micro)),
            pltpu.SemaphoreType.DMA((2, micro)),
        ],
        compiler_params=pltpu.CompilerParams(
            collective_id=0, has_side_effects=True, vmem_limit_bytes=60 * 2**20
        ),
    )(
        inputs, cotangent, gain, route[0], jnp.swapaxes(route[0], 1, 2), gate[0],
        w_gate[0, 0], w_up[0, 0], w_down[0, 0],
    )
    return (hidden[None], grads[None])


def solution(mesh):
    placed = (
        P(None, "expert", None),
        P(None, "expert", None),
        P("section", None),
        P("section", None, "expert", None),
        P("section", None, "expert", None),
        P("section", "expert", None, None),
        P("section", "expert", None, None),
        P("section", "expert", None, None),
    )
    return jax.shard_map(
        local,
        mesh=mesh,
        in_specs=placed,
        out_specs=(P("section", None, "expert", None), P("section", None, "expert", None)),
        check_vma=False,
    )
```

time: 1170 us -> 399 us (0.34)
  waiting for transfers between devices: 700 us -> 0 us
  Pallas kernels: 0 us -> 391 us
  starting transfers between devices: 138 us -> 0 us
  local copies, waits for them, and re-layouts: 140 us -> 7.41 us
  matrix products: 92.5 us -> 0 us
  other arithmetic: 79.3 us -> 0 us
  loops' own time: 11.9 us -> 0 us
    all_to_all x28 -> x0, waiting for transfers between devices: 587 us -> none  [the longest x14 268 us: return_rows(): lax.all_to_all(rows, 'expert', split_axis=0, concat_axis=0, tiled=True)]
    pallas_call x0 -> x1, Pallas kernels: none -> 391 us  [local(): pl.pallas_call(functools.partial(kernel, experts, sections, capacity), ou...]
    ppermute x14 -> x0, waiting for transfers between devices: 114 us -> none  [passed_along(): lax.ppermute(value, axis, [(source, source + steps) for source in range(l...]
    all_to_all x28 -> x0, starting transfers between devices: 112 us -> none  [the longest x14 55.8 us: return_rows(): lax.all_to_all(rows, 'expert', split_axis=0, concat_axis=0, tiled=True)]
    dot_general x38 -> x0, matrix products: 92.5 us -> none  [the longest x12 50.9 us: contract_last(): lax.dot_general(left, right, (((1,), (1,)), ((), ())), preferred_element_...]
    dynamic_slice x81 -> x0, local copies, waits for them, and re-layouts: 57.6 us -> none  [the longest x7 11.8 us: forward_tick(): old_out = lax.dynamic_index_in_dim(outputs, index, 0, keepdims=False)]
    dynamic_update_slice x28 -> x0, other arithmetic: 38.1 us -> none  [the longest x7 13.2 us: backward_tick(): lax.dynamic_update_index_in_dim(results, jnp.where(live, result, old_resu...]
    reshape x52 -> x0, local copies, waits for them, and re-layouts: 36 us -> none  [the longest x7 8.53 us: backward_work(): grad_send = grad_send.reshape(experts, capacity, width)]
  transfers between devices with their start and end apart: 42 -> 0, of which waited for: 42 -> 0; matrix products, arithmetic and copies ran while one was open for 4% -> 0% of each run, Pallas kernels for 0% -> 0%
where the time goes in v1:
time: 399 us
  Pallas kernels  391 us (98%)
  local copies, waits for them, and re-layouts  7.41 us (2%)
    pallas_call x1, Pallas kernels, local(): pl.pallas_call(functools.partial(kernel, experts, sections, capacity), ou...  391 us

profile of v1, /device:TPU:0, one launch (start us, length us, event | category | flops | bytes accessed | tf_op | source)
XLA Modules:
  0.0 399.0 jit_solution(4376187967752544079)
XLA Ops:
  0.6 1.4 copy.10
  2.0 1.4 copy.11.route
  3.5 391.0 %shard_map.95 = (bf16[4,32,4096]{2,1,0:T(8,128)(2,1)}, bf16[4,32,4096]{2,1,0:T(8,128)(2,1)}) custom-call(bf16[4,32,4096]{2,1,0:T(8,128)(2,1)} %inputs.1, bf16[4,32,4096]{2,1,0:T(8,128)(2,1)} %cotangent.1, f32[1,4096]{1,0:T(1,128)} %gain.1, s32[4,32,2]{2,1,0:T(8,128)} %copy.11.route, s32[4,2,32]{2,1,0:T(2,128)} %bitcast.16, f32[4,32,2]{2,1,0:T(8,128)} %bitcast.14, ...), custom_call_target="tpu_custom_call" | custom-call | tf_op jit(solution)/shard_map/pallas_call | solution.py:358
  394.4 2.3 copy.14
  396.7 2.3 copy.15

commit v2 on v1

v2 whole, which is shorter than its diff:
```python
import functools

import jax
import jax.numpy as jnp
from jax import lax
from jax.experimental import pallas as pl
from jax.experimental.pallas import tpu as pltpu
from jax.sharding import PartitionSpec as P

EPS = 1e-06
MESH = pl.DeviceIdType.MESH
FOLD = 16
PARTS = 2
F32 = jnp.float32
BF16 = jnp.bfloat16


def mm(left, right):
    return jnp.dot(left, right, preferred_element_type=F32)


def mm_last(left, right):
    return lax.dot_general(left, right, (((1,), (1,)), ((), ())), preferred_element_type=F32)


def onehot(condition):
    return jnp.where(condition, 1.0, 0.0).astype(F32)


def kernel(
    experts, sections, capacity,
    inputs, cotangent, gain, routing, w_gate, w_up, w_down,
    hidden, grads,
    wg, wu, wd, xin, dyin, sent, got, kept_gate, kept_up, d_inner, wide, narrow,
    inner_p, inner_a, inner_b, pick, place,
    weight_sem, send_sem, recv_sem, pass_send, pass_recv,
):
    micro, tok, width = inputs.shape
    inner = wg.shape[1]
    rows = experts * capacity
    block = capacity * FOLD
    part_width = width // PARTS
    piece = part_width // FOLD
    section = lax.axis_index("section")
    me = lax.axis_index("expert")
    last = section == sections - 1
    parts = [slice(h * part_width, (h + 1) * part_width) for h in range(PARTS)]

    weight_copies = [
        pltpu.make_async_copy(source, target, weight_sem.at[i])
        for i, (source, target) in enumerate(((w_gate, wg), (w_up, wu), (w_down, wd)))
    ]
    for copy in weight_copies:
        copy.start()

    barrier = pltpu.get_barrier_semaphore()
    for d in range(1, experts):
        pl.semaphore_signal(
            barrier, inc=1, device_id={"expert": lax.rem(me + d, experts)}, device_id_type=MESH
        )
    for d in (1, sections - 1):
        pl.semaphore_signal(
            barrier, inc=1, device_id={"section": lax.rem(section + d, sections)},
            device_id_type=MESH,
        )

    @pl.when(section == 0)
    def _():
        xin[...] = inputs[...]

    @pl.when(last)
    def _():
        dyin[...] = cotangent[...]

    every = micro * tok
    expert_i = lax.broadcasted_iota(jnp.int32, (every, experts), 1).astype(F32)
    ohs = [onehot(routing[:, k:k + 1] == expert_i) for k in range(2)]
    row_t = lax.broadcasted_iota(jnp.int32, (every, every), 0)
    col_t = lax.broadcasted_iota(jnp.int32, (every, every), 1)
    earlier = onehot((col_t < row_t) & (col_t // tok == row_t // tok))
    before = mm(earlier.astype(BF16), (ohs[0] + ohs[1]).astype(BF16))
    slot = lax.broadcasted_iota(jnp.int32, (every, 128), 1).astype(F32)
    for k in range(2):
        at_row = routing[:, k:k + 1] * capacity + jnp.sum(
            ohs[k] * before, axis=1, keepdims=True
        )
        table = onehot(slot == at_row)
        table_t = table.T
        for m in range(micro):
            pick[k, m] = table[m * tok:(m + 1) * tok, :rows].astype(BF16)
            place[k, m] = table_t[:rows, m * tok:(m + 1) * tok].astype(BF16)

    pl.semaphore_wait(barrier, experts + 1)

    def rows_of(e):
        return pl.ds(pl.multiple_of(e * block, 16), block)

    def exchange(kind, m, h, peer):
        return pltpu.make_async_remote_copy(
            src_ref=sent.at[kind, m, h, rows_of(peer)],
            dst_ref=got.at[kind, m, h, rows_of(me)],
            send_sem=send_sem.at[kind, m, h, peer],
            recv_sem=recv_sem.at[kind, m, h, me],
            device_id={"expert": peer},
            device_id_type=MESH,
        )

    def arrival(kind, m, h, peer):
        return pltpu.make_async_remote_copy(
            src_ref=sent.at[kind, m, h, rows_of(me)],
            dst_ref=got.at[kind, m, h, rows_of(peer)],
            send_sem=send_sem.at[kind, m, h, me],
            recv_sem=recv_sem.at[kind, m, h, peer],
            device_id={"expert": peer},
            device_id_type=MESH,
        )

    def hidden_pass(m, h):
        return pltpu.make_async_remote_copy(
            src_ref=hidden.at[m, :, parts[h]], dst_ref=xin.at[m, :, parts[h]],
            send_sem=pass_send.at[0, m, h], recv_sem=pass_recv.at[0, m, h],
            device_id={"section": lax.rem(section + 1, sections)}, device_id_type=MESH,
        )

    def grads_pass(m, h):
        return pltpu.make_async_remote_copy(
            src_ref=grads.at[m, :, parts[h]], dst_ref=dyin.at[m, :, parts[h]],
            send_sem=pass_send.at[1, m, h], recv_sem=pass_recv.at[1, m, h],
            device_id={"section": lax.rem(section + sections - 1, sections)},
            device_id_type=MESH,
        )

    span = 8 * FOLD
    row_i = lax.broadcasted_iota(jnp.int32, (span, span), 0)
    col_i = lax.broadcasted_iota(jnp.int32, (span, span), 1)

    def ship(kind, m, h):
        order = onehot(col_i == (row_i % FOLD) * 8 + row_i // FOLD).astype(BF16)

        def step(g, _):
            at = pl.ds(pl.multiple_of(g * 8, 8), 8)
            base = h * part_width
            stack = jnp.concatenate(
                [wide[at, base + p * piece:base + (p + 1) * piece] for p in range(FOLD)], axis=0
            ).astype(BF16)
            sent[kind, m, h, pl.ds(pl.multiple_of(g * span, span), span), :] = mm(
                order, stack
            ).astype(BF16)
            return 0

        lax.fori_loop(0, rows // 8, step, 0, unroll=True)
        for d in range(1, experts):
            exchange(kind, m, h, lax.rem(me + d, experts)).start()
        got[kind, m, h, rows_of(me), :] = sent[kind, m, h, rows_of(me), :]

    def collect(kind, m, h):
        for d in range(1, experts):
            arrival(kind, m, h, lax.rem(me + d, experts)).wait_recv()
        order = onehot(col_i == (row_i % 8) * FOLD + row_i // 8).astype(BF16)

        def step(g, _):
            at = pl.ds(pl.multiple_of(g * 8, 8), 8)
            base = h * part_width
            flat = mm(order, got[kind, m, h, pl.ds(pl.multiple_of(g * span, span), span), :])
            for p in range(FOLD):
                wide[at, base + p * piece:base + (p + 1) * piece] = flat[p * 8:(p + 1) * 8]
            return 0

        lax.fori_loop(0, rows // 8, step, 0, unroll=True)
        narrow[:, parts[h]] = wide[:, parts[h]].astype(BF16)

    def rms_of(values):
        return lax.rsqrt(jnp.mean(values * values, axis=-1, keepdims=True) + EPS)

    def gates_of(m):
        weights = routing[pl.ds(pl.multiple_of(m * tok, 8), tok), :]
        return [weights[:, 2 + k:3 + k] for k in range(2)]

    def forward_send(m):
        @pl.when(section > 0)
        def _():
            for h in range(PARTS):
                hidden_pass(m, h).wait_recv()

        values = xin[m].astype(F32)
        normed = (values * rms_of(values) * gain[...]).astype(BF16)
        table = place[0, m] + place[1, m]
        for h in range(PARTS):
            wide[:, parts[h]] = mm(table, normed[:, parts[h]])
            ship(0, m, h)

    def forward_up(m):
        @pl.when(m == 0)
        def _():
            for copy in weight_copies:
                copy.wait()

        for h in range(PARTS):
            collect(0, m, h)

            def up(n, _):
                at = pl.ds(pl.multiple_of(n * 256, 256), 256)
                pre_gate = mm(narrow[:, parts[h]], wg[parts[h], at])
                pre_up = mm(narrow[:, parts[h]], wu[parts[h], at])
                if h > 0:
                    pre_gate = kept_gate[m, :, at] + pre_gate
                    pre_up = kept_up[m, :, at] + pre_up
                kept_gate[m, :, at] = pre_gate
                kept_up[m, :, at] = pre_up
                if h == PARTS - 1:
                    inner_p[:, at] = (
                        pre_gate * jax.nn.sigmoid(pre_gate) * pre_up
                    ).astype(BF16)
                return 0

            lax.fori_loop(0, inner // 256, up, 0, unroll=True)

    def forward_down(m):
        for h in range(PARTS):
            def down(n, _):
                at = pl.ds(pl.multiple_of(h * part_width + n * 512, 512), 512)
                wide[:, at] = mm(inner_p[...], wd[:, at])
                return 0

            lax.fori_loop(0, part_width // 512, down, 0, unroll=True)
            ship(1, m, h)

    def forward_merge(m):
        gates = gates_of(m)
        for h in range(PARTS):
            collect(1, m, h)
            mixed = (
                xin[m, :, parts[h]].astype(F32)
                + gates[0] * mm(pick[0, m], narrow[:, parts[h]])
                + gates[1] * mm(pick[1, m], narrow[:, parts[h]])
            )
            hidden[m, :, parts[h]] = mixed.astype(BF16)

            @pl.when(section < sections - 1)
            def _():
                hidden_pass(m, h).start()

    def backward_send(m):
        gates = gates_of(m)
        table = jnp.concatenate(
            [place[0, m].astype(F32), place[1, m].astype(F32)], axis=1
        ).astype(BF16)
        for h in range(PARTS):
            @pl.when(section < sections - 1)
            def _():
                grads_pass(m, h).wait_recv()

            grad_out = dyin[m, :, parts[h]].astype(F32)
            scaled = jnp.concatenate(
                [(gates[k] * grad_out).astype(BF16) for k in range(2)], axis=0
            )
            wide[:, parts[h]] = mm(table, scaled)
            ship(2, m, h)

    def backward_expert(m):
        for h in range(PARTS):
            collect(2, m, h)

            def down(n, _):
                at = pl.ds(pl.multiple_of(n * 256, 256), 256)
                d_hidden = mm_last(narrow[:, parts[h]], wd[at, parts[h]])
                if h > 0:
                    d_hidden = d_inner[:, at] + d_hidden
                if h < PARTS - 1:
                    d_inner[:, at] = d_hidden
                else:
                    pre_gate = kept_gate[m, :, at]
                    pre_up = kept_up[m, :, at]
                    sigma = jax.nn.sigmoid(pre_gate)
                    inner_a[:, at] = (
                        d_hidden * pre_up * sigma * (1.0 + pre_gate * (1.0 - sigma))
                    ).astype(BF16)
                    inner_b[:, at] = (d_hidden * pre_gate * sigma).astype(BF16)
                return 0

            lax.fori_loop(0, inner // 256, down, 0, unroll=True)

        for h in range(PARTS):
            def up(n, _):
                at = pl.ds(pl.multiple_of(h * part_width + n * 512, 512), 512)
                wide[:, at] = mm_last(inner_a[...], wg[at, :]) + mm_last(inner_b[...], wu[at, :])
                return 0

            lax.fori_loop(0, part_width // 512, up, 0, unroll=True)
            ship(3, m, h)

    def backward_merge(m):
        values = xin[m].astype(F32)
        scale = rms_of(values)
        table = pick[0, m] + pick[1, m]
        weighted = []
        for h in range(PARTS):
            collect(3, m, h)
            weighted.append(mm(table, narrow[:, parts[h]]) * gain[:, parts[h]])
        total = sum(
            jnp.sum(values[:, parts[h]] * weighted[h], axis=-1, keepdims=True)
            for h in range(PARTS)
        )
        factor = scale * scale * scale * (total * (1.0 / width))
        for h in range(PARTS):
            result = (
                dyin[m, :, parts[h]].astype(F32)
                + scale * weighted[h]
                - values[:, parts[h]] * factor
            )
            grads[m, :, parts[h]] = result.astype(BF16)

            @pl.when(section > 0)
            def _():
                grads_pass(m, h).start()

    @pl.when(last)
    def _():
        def early(m, _):
            backward_send(m)
            return 0

        lax.fori_loop(0, micro, early, 0)

    def tick(t, _):
        ahead = t - section
        back = t - (2 * sections - 2 - section)
        go_ahead = (ahead >= 0) & (ahead < micro)
        go_back = (back >= 0) & (back < micro)
        others = section < sections - 1

        def guarded(condition, stage, m):
            @pl.when(condition)
            def _():
                stage(m)

        guarded(go_ahead, forward_send, ahead)
        guarded(go_ahead, forward_up, ahead)
        guarded(go_ahead & others, forward_down, ahead)
        guarded(go_back & others, backward_send, back)
        guarded(go_ahead & others, forward_merge, ahead)
        guarded(go_back, backward_expert, back)
        guarded(go_ahead & last, forward_down, ahead)
        guarded(go_back, backward_merge, back)
        guarded(go_ahead & last, forward_merge, ahead)
        return 0

    lax.fori_loop(0, 2 * sections + micro - 2, tick, 0)

    def drain(m, _):
        for h in range(PARTS):
            for kind in range(4):
                for d in range(1, experts):
                    exchange(kind, m, h, lax.rem(me + d, experts)).wait_send()

            @pl.when(section < sections - 1)
            def _():
                hidden_pass(m, h).wait_send()

            @pl.when(section > 0)
            def _():
                grads_pass(m, h).wait_send()

        return 0

    lax.fori_loop(0, micro, drain, 0)


def local(inputs, cotangent, gain, route, gate, w_gate, w_up, w_down):
    micro, tok, width = inputs.shape
    top = route.shape[-1]
    experts = lax.axis_size("expert")
    sections = lax.axis_size("section")
    capacity = tok * top * 7 // (6 * experts)
    rows = experts * capacity
    inner = w_gate.shape[-1]
    vmem = pl.BlockSpec(memory_space=pltpu.VMEM)
    hbm = pl.BlockSpec(memory_space=pl.ANY)
    shape = jax.ShapeDtypeStruct((micro, tok, width), BF16)
    routing = jnp.concatenate([route[0].astype(F32), gate[0]], axis=-1).reshape(micro * tok, 2 * top)
    hidden, grads = pl.pallas_call(
        functools.partial(kernel, experts, sections, capacity),
        out_shape=(shape, shape),
        in_specs=[vmem] * 4 + [hbm] * 3,
        out_specs=(vmem, vmem),
        scratch_shapes=[
            pltpu.VMEM((width, inner), BF16),
            pltpu.VMEM((width, inner), BF16),
            pltpu.VMEM((inner, width), BF16),
            pltpu.VMEM((micro, tok, width), BF16),
            pltpu.VMEM((micro, tok, width), BF16),
            pltpu.VMEM((4, micro, PARTS, rows * FOLD, width // PARTS // FOLD), BF16),
            pltpu.VMEM((4, micro, PARTS, rows * FOLD, width // PARTS // FOLD), BF16),
            pltpu.VMEM((micro, rows, inner), F32),
            pltpu.VMEM((micro, rows, inner), F32),
            pltpu.VMEM((rows, inner), F32),
            pltpu.VMEM((rows, width), F32),
            pltpu.VMEM((rows, width), BF16),
            pltpu.VMEM((rows, inner), BF16),
            pltpu.VMEM((rows, inner), BF16),
            pltpu.VMEM((rows, inner), BF16),
            pltpu.VMEM((2, micro, tok, rows), BF16),
            pltpu.VMEM((2, micro, rows, tok), BF16),
            pltpu.SemaphoreType.DMA((3,)),
            pltpu.SemaphoreType.DMA((4, micro, PARTS, experts)),
            pltpu.SemaphoreType.DMA((4, micro, PARTS, experts)),
            pltpu.SemaphoreType.DMA((2, micro, PARTS)),
            pltpu.SemaphoreType.DMA((2, micro, PARTS)),
        ],
        compiler_params=pltpu.CompilerParams(
            collective_id=0, has_side_effects=True, vmem_limit_bytes=60 * 2**20
        ),
    )(
        inputs, cotangent, gain, routing,
        w_gate[0, 0], w_up[0, 0], w_down[0, 0],
    )
    return (hidden[None], grads[None])


def solution(mesh):
    placed = (
        P(None, "expert", None),
        P(None, "expert", None),
        P("section", None),
        P("section", None, "expert", None),
        P("section", None, "expert", None),
        P("section", "expert", None, None),
        P("section", "expert", None, None),
        P("section", "expert", None, None),
    )
    return jax.shard_map(
        local,
        mesh=mesh,
        in_specs=placed,
        out_specs=(P("section", None, "expert", None), P("section", None, "expert", None)),
        check_vma=False,
    )
```

time: 399 us -> 361 us (0.905)
  Pallas kernels: 391 us -> 353 us
    pallas_call x1, Pallas kernels: 391 us -> 353 us  [local(): pl.pallas_call(functools.partial(kernel, experts, sections, capacity), ou...]
where the time goes in v2:
time: 361 us
  Pallas kernels  353 us (98%)
  local copies, waits for them, and re-layouts  6.18 us (2%)
    pallas_call x1, Pallas kernels, local(): pl.pallas_call(functools.partial(kernel, experts, sections, capacity), ou...  353 us

profile of v2, /device:TPU:0, one launch (start us, length us, event | category | flops | bytes accessed | tf_op | source)
XLA Modules:
  0.0 360.5 jit_solution(76913112411463337)
XLA Ops:
  0.6 0.7 convert_element_type.7
  1.3 0.1 convert_element_type.8
  1.4 0.7 copy.13
  2.1 0.1 concatenate.6
  2.2 0.7 copy.14.routing
  2.9 353.0 %shard_map.95 = (bf16[4,32,4096]{2,1,0:T(8,128)(2,1)}, bf16[4,32,4096]{2,1,0:T(8,128)(2,1)}) custom-call(bf16[4,32,4096]{2,1,0:T(8,128)(2,1)} %inputs.1, bf16[4,32,4096]{2,1,0:T(8,128)(2,1)} %cotangent.1, f32[1,4096]{1,0:T(1,128)} %gain.1, f32[128,4]{1,0:T(8,128)} %copy.14.routing, bf16[4096,768]{1,0:T(8,128)(2,1)} %bitcast.9, bf16[4096,768]{1,0:T(8,128)(2,1)} %bitcast.10, ...), custom_call_target="tpu_custom_call" | custom-call | tf_op jit(solution)/shard_map/pallas_call | solution.py:381
  355.9 2.3 copy.17
  358.2 2.3 copy.18
  (2 shorter events, 0.0 us)

commit v3 on v2

--- a/solution.py
+++ b/solution.py
@@ -323,8 +323,8 @@
         lax.fori_loop(0, micro, early, 0)
 
     def tick(t, _):
-        ahead = t - section
-        back = t - (2 * sections - 2 - section)
+        ahead = t - 1
+        back = jnp.where(last, ahead, ahead - micro)
         go_ahead = (ahead >= 0) & (ahead < micro)
         go_back = (back >= 0) & (back < micro)
         others = section < sections - 1
@@ -334,18 +334,17 @@
             def _():
                 stage(m)
 
-        guarded(go_ahead, forward_send, ahead)
         guarded(go_ahead, forward_up, ahead)
         guarded(go_ahead & others, forward_down, ahead)
         guarded(go_back & others, backward_send, back)
-        guarded(go_ahead & others, forward_merge, ahead)
         guarded(go_back, backward_expert, back)
         guarded(go_ahead & last, forward_down, ahead)
+        guarded(t < micro, forward_send, t)
         guarded(go_back, backward_merge, back)
-        guarded(go_ahead & last, forward_merge, ahead)
+        guarded(go_ahead, forward_merge, ahead)
         return 0
 
-    lax.fori_loop(0, 2 * sections + micro - 2, tick, 0)
+    lax.fori_loop(0, 2 * micro + 1, tick, 0)
 
     def drain(m, _):
         for h in range(PARTS):

time: 361 us -> 373 us (1.033)
  Pallas kernels: 353 us -> 365 us
    pallas_call x1, Pallas kernels: 353 us -> 365 us  [local(): pl.pallas_call(functools.partial(kernel, experts, sections, capacity), ou...]
where the time goes in v3:
time: 373 us
  Pallas kernels  365 us (98%)
  local copies, waits for them, and re-layouts  6.18 us (2%)
    pallas_call x1, Pallas kernels, local(): pl.pallas_call(functools.partial(kernel, experts, sections, capacity), ou...  365 us

profile of v3, /device:TPU:0, one launch (start us, length us, event | category | flops | bytes accessed | tf_op | source)
XLA Modules:
  0.0 372.9 jit_solution(13017352140779333717)
XLA Ops:
  0.6 0.7 convert_element_type.7
  1.3 0.1 convert_element_type.8
  1.4 0.7 copy.13
  2.1 0.1 concatenate.6
  2.2 0.7 copy.14.routing
  2.9 365.3 %shard_map.95 = (bf16[4,32,4096]{2,1,0:T(8,128)(2,1)}, bf16[4,32,4096]{2,1,0:T(8,128)(2,1)}) custom-call(bf16[4,32,4096]{2,1,0:T(8,128)(2,1)} %inputs.1, bf16[4,32,4096]{2,1,0:T(8,128)(2,1)} %cotangent.1, f32[1,4096]{1,0:T(1,128)} %gain.1, f32[128,4]{1,0:T(8,128)} %copy.14.routing, bf16[4096,768]{1,0:T(8,128)(2,1)} %bitcast.9, bf16[4096,768]{1,0:T(8,128)(2,1)} %bitcast.10, ...), custom_call_target="tpu_custom_call" | custom-call | tf_op jit(solution)/shard_map/pallas_call | solution.py:380
  368.3 2.3 copy.17
  370.6 2.3 copy.18
  (2 shorter events, 0.0 us)

commit v4 on v2

--- a/solution.py
+++ b/solution.py
@@ -334,13 +334,14 @@
             def _():
                 stage(m)
 
-        guarded(go_ahead, forward_send, ahead)
+        guarded(go_ahead & others, forward_send, ahead)
         guarded(go_ahead, forward_up, ahead)
         guarded(go_ahead & others, forward_down, ahead)
         guarded(go_back & others, backward_send, back)
         guarded(go_ahead & others, forward_merge, ahead)
         guarded(go_back, backward_expert, back)
         guarded(go_ahead & last, forward_down, ahead)
+        guarded((ahead >= -1) & (ahead < micro - 1) & last, forward_send, ahead + 1)
         guarded(go_back, backward_merge, back)
         guarded(go_ahead & last, forward_merge, ahead)
         return 0

time: 361 us -> 363 us (level)
  no operation moved by 1% of the time
where the time goes in v4:
time: 363 us
  Pallas kernels  355 us (98%)
  local copies, waits for them, and re-layouts  6.18 us (2%)
    pallas_call x1, Pallas kernels, local(): pl.pallas_call(functools.partial(kernel, experts, sections, capacity), ou...  355 us

profile of v4, /device:TPU:0, one launch (start us, length us, event | category | flops | bytes accessed | tf_op | source)
XLA Modules:
  0.0 362.6 jit_solution(3014836946246663818)
XLA Ops:
  0.6 0.7 convert_element_type.7
  1.3 0.1 convert_element_type.8
  1.4 0.7 copy.13
  2.1 0.1 concatenate.6
  2.2 0.7 copy.14.routing
  2.9 355.0 %shard_map.95 = (bf16[4,32,4096]{2,1,0:T(8,128)(2,1)}, bf16[4,32,4096]{2,1,0:T(8,128)(2,1)}) custom-call(bf16[4,32,4096]{2,1,0:T(8,128)(2,1)} %inputs.1, bf16[4,32,4096]{2,1,0:T(8,128)(2,1)} %cotangent.1, f32[1,4096]{1,0:T(1,128)} %gain.1, f32[128,4]{1,0:T(8,128)} %copy.14.routing, bf16[4096,768]{1,0:T(8,128)(2,1)} %bitcast.9, bf16[4096,768]{1,0:T(8,128)(2,1)} %bitcast.10, ...), custom_call_target="tpu_custom_call" | custom-call | tf_op jit(solution)/shard_map/pallas_call | solution.py:382
  358.0 2.3 copy.17
  360.3 2.3 copy.18
  (2 shorter events, 0.0 us)

commit v5 on v4

--- a/solution.py
+++ b/solution.py
@@ -324,7 +324,7 @@
 
     def tick(t, _):
         ahead = t - section
-        back = t - (2 * sections - 2 - section)
+        back = jnp.where(last, ahead, ahead - micro)
         go_ahead = (ahead >= 0) & (ahead < micro)
         go_back = (back >= 0) & (back < micro)
         others = section < sections - 1
@@ -346,7 +346,7 @@
         guarded(go_ahead & last, forward_merge, ahead)
         return 0
 
-    lax.fori_loop(0, 2 * sections + micro - 2, tick, 0)
+    lax.fori_loop(0, sections - 1 + 2 * micro, tick, 0)
 
     def drain(m, _):
         for h in range(PARTS):
@@ -365,6 +365,17 @@
         return 0
 
     lax.fori_loop(0, micro, drain, 0)
+
+
+def place_outputs(hidden, grads, hidden_out, grads_out, sem):
+    copies = [
+        pltpu.make_async_copy(hidden, hidden_out, sem.at[0]),
+        pltpu.make_async_copy(grads, grads_out, sem.at[1]),
+    ]
+    for copy in copies:
+        copy.start()
+    for copy in copies:
+        copy.wait()
 
 
 def local(inputs, cotangent, gain, route, gate, w_gate, w_up, w_down):
@@ -415,6 +426,13 @@
         inputs, cotangent, gain, routing,
         w_gate[0, 0], w_up[0, 0], w_down[0, 0],
     )
+    hidden, grads = pl.pallas_call(
+        place_outputs,
+        out_shape=(shape, shape),
+        in_specs=[hbm] * 2,
+        out_specs=(hbm, hbm),
+        scratch_shapes=[pltpu.SemaphoreType.DMA((2,))],
+    )(hidden, grads)
     return (hidden[None], grads[None])
 
 

time: 363 us -> 436 us (1.20)
  Pallas kernels: 355 us -> 432 us
  local copies, waits for them, and re-layouts: 6.18 us -> 1.61 us
    pallas_call x0 -> x1, Pallas kernels: none -> 64.6 us  [local(): pl.pallas_call(place_outputs, out_shape=(shape, shape), in_specs=[hbm] *...]
    pallas_call x1, Pallas kernels: 355 us -> 368 us  [local(): pl.pallas_call(functools.partial(kernel, experts, sections, capacity), ou...]
    unnamed x3 -> x1, local copies, waits for them, and re-layouts: 5.26 us -> 0.69 us
where the time goes in v5:
time: 436 us; the launch traced here: 435 us
  Pallas kernels  432 us (99%)
    pallas_call x1, Pallas kernels, local(): pl.pallas_call(functools.partial(kernel, experts, sections, capacity), ou...  368 us
    pallas_call x1, Pallas kernels, local(): pl.pallas_call(place_outputs, out_shape=(shape, shape), in_specs=[hbm] *...  64.6 us

profile of v5, /device:TPU:0, one launch (start us, length us, event | category | flops | bytes accessed | tf_op | source)
XLA Modules:
  0.0 435.4 jit_solution(17605756666789494525)
XLA Ops:
  0.6 0.7 convert_element_type.7
  1.3 0.1 convert_element_type.8
  1.4 0.7 copy.13
  2.1 0.1 concatenate.6
  2.2 0.7 copy.14.routing
  2.9 367.8 %shard_map.95 = (bf16[4,32,4096]{2,1,0:T(8,128)(2,1)}, bf16[4,32,4096]{2,1,0:T(8,128)(2,1)}) custom-call(bf16[4,32,4096]{2,1,0:T(8,128)(2,1)} %inputs.1, bf16[4,32,4096]{2,1,0:T(8,128)(2,1)} %cotangent.1, f32[1,4096]{1,0:T(1,128)} %gain.1, f32[128,4]{1,0:T(8,128)} %copy.14.routing, bf16[4096,768]{1,0:T(8,128)(2,1)} %bitcast.9, bf16[4096,768]{1,0:T(8,128)(2,1)} %bitcast.10, ...), custom_call_target="tpu_custom_call" | custom-call | tf_op jit(solution)/shard_map/pallas_call | solution.py:393
  370.7 64.6 %shard_map.96 = (bf16[4,32,4096]{2,1,0:T(8,128)(2,1)}, bf16[4,32,4096]{2,1,0:T(8,128)(2,1)}) custom-call(bf16[4,32,4096]{2,1,0:T(8,128)(2,1)} %get-tuple-element.6.hidden, bf16[4,32,4096]{2,1,0:T(8,128)(2,1)} %get-tuple-element.7.grads), custom_call_target="tpu_custom_call" | custom-call | tf_op jit(solution)/shard_map/pallas_call | solution.py:429
  (2 shorter events, 0.0 us)
